TPU v7x, 32 devices: a whole 2x2x4 slice. The times are simulated.
32 devices in a mesh: groups: 2 (over x), gx: 8 (over z, y), gy: 2 (over core).
Axes of the slice: x: 2, y: 2, z: 4, core: 2. Of those that a mesh axis runs over, the one named last changes fastest.
Arguments:
- field: bfloat16 [512, 256, 8, 128], P(('groups', 'gx'), 'gy'), parts along dimension 0, may hold values from -6 to 6
- cotangent: bfloat16 [512, 256, 8, 128], P(('groups', 'gx'), 'gy'), parts along dimension 0, may hold values from -6 to 6
- spectral_weight: bfloat16 [24, 192, 64, 128], P(None, ('gx', 'gy')), may hold values from -6 to 6
- mix_weight: bfloat16 [64, 64], replicated, may hold values from -0.75 to 0.75
Outputs:
- mixed: bfloat16 [512, 256, 8, 128], P(('groups', 'gx'), 'gy'), parts along dimension 0
- field_grad: bfloat16 [512, 256, 8, 128], P(('groups', 'gx'), 'gy'), parts along dimension 0
- spectral_grad: float32 [48, 192, 64, 128], P('groups', ('gx', 'gy')), parts along dimension 0
- mix_grad: float32 [128, 64], P('groups'), parts along dimension 0
There are 2 independent parts, one for each index of `groups`. A program takes and returns all parts, laid end to end along the dimension named above; an argument that names none is the same for every part. Nothing has to cross between parts.
All inputs are finite; a program needn't handle non-finite values.
Results may differ from a plain program's by a relative error of at most 0.0079.
Values may be sent and summed in bfloat16 or wider, within the bound.
A program may use at most 384 MiB of HBM per device.

v0:
```python
import math

import jax
import jax.numpy as jnp
from jax import lax
from jax.sharding import PartitionSpec as P


def wave_tables(length, modes, offset, count):
    index = jnp.arange(modes, dtype=jnp.int32)
    freqs = jnp.where(index < modes // 2, index, index - modes)
    places = offset + jnp.arange(count, dtype=jnp.int32)
    phase = freqs[:, None] * places[None, :] % length
    angle = phase.astype(jnp.float32) * (2.0 * math.pi / length)
    factor = 1.0 / math.sqrt(length)
    return (
        (jnp.cos(angle) * factor).astype(jnp.bfloat16),
        (jnp.sin(angle) * factor).astype(jnp.bfloat16),
    )


def fold_forward(first, second, half):
    real = first[..., :half] + second[..., half:]
    imag = first[..., half:] - second[..., :half]
    return jnp.concatenate([real, imag], axis=-1)


def fold_inverse(first, second, half):
    real = first[..., :half] - second[..., half:]
    imag = first[..., half:] + second[..., :half]
    return jnp.concatenate([real, imag], axis=-1)


def on_device(field, cotangent, spectral_weight, mix_weight):
    x_cells, y_cells, pair_count, doubled = field.shape
    channels = doubled // 2
    modes = spectral_weight.shape[0]
    x_devices = lax.axis_size("gx")
    total_x = x_cells * x_devices
    total_y = y_cells * lax.axis_size("gy")
    x_start = lax.axis_index("gx") * x_cells
    y_start = lax.axis_index("gy") * y_cells
    cos_y, sin_y = wave_tables(total_y, modes, y_start, y_cells)

    def transform_rows(data):
        first = jnp.einsum("ky,xyps->kpxs", cos_y, data, preferred_element_type=jnp.float32)
        second = jnp.einsum("ky,xyps->kpxs", sin_y, data, preferred_element_type=jnp.float32)
        folded = fold_forward(first, second, channels)
        return folded.reshape(x_devices, -1, x_cells, doubled)

    stacked = jnp.stack([transform_rows(field), transform_rows(cotangent)], axis=1)
    narrow = lax.psum_scatter(stacked, "gy", scatter_dimension=2, tiled=True).astype(jnp.bfloat16)
    cos_local, sin_local = wave_tables(total_x, modes, x_start, x_cells)
    piece = narrow
    first = jnp.einsum("kx,ifmxs->ifmks", cos_local, piece, preferred_element_type=jnp.float32)
    second = jnp.einsum("kx,ifmxs->ifmks", sin_local, piece, preferred_element_type=jnp.float32)
    spectrum = lax.psum_scatter(
        fold_forward(first, second, channels), "gx", scatter_dimension=0, tiled=True
    ).astype(jnp.bfloat16)
    hat_field = spectrum[0, 0]
    hat_cotangent = spectrum[0, 1]
    first = jnp.einsum(
        "lkc,klcs->lks",
        hat_field[..., :channels],
        spectral_weight,
        preferred_element_type=jnp.float32,
    )
    second = jnp.einsum(
        "lkc,klcs->lks",
        hat_field[..., channels:],
        spectral_weight,
        preferred_element_type=jnp.float32,
    )
    out_modes = fold_inverse(first, second, channels).astype(jnp.bfloat16)
    swapped = jnp.concatenate(
        [hat_cotangent[..., channels:], -hat_cotangent[..., :channels]], axis=-1
    )
    back_modes = jnp.concatenate(
        [
            jnp.einsum(
                "lks,klcs->lkc", hat_cotangent, spectral_weight, preferred_element_type=jnp.float32
            ),
            jnp.einsum(
                "lks,klcs->lkc", swapped, spectral_weight, preferred_element_type=jnp.float32
            ),
        ],
        axis=-1,
    ).astype(jnp.bfloat16)
    field_real, field_imag = (hat_field[..., :channels], hat_field[..., channels:])
    cot_real, cot_imag = (hat_cotangent[..., :channels], hat_cotangent[..., channels:])
    grad_real = jnp.einsum(
        "lkc,lko->klco", field_real, cot_real, preferred_element_type=jnp.float32
    ) + jnp.einsum("lkc,lko->klco", field_imag, cot_imag, preferred_element_type=jnp.float32)
    grad_imag = jnp.einsum(
        "lkc,lko->klco", field_real, cot_imag, preferred_element_type=jnp.float32
    ) - jnp.einsum("lkc,lko->klco", field_imag, cot_real, preferred_element_type=jnp.float32)
    spectral_grad = jnp.concatenate([grad_real, grad_imag], axis=-1)
    outgoing = jnp.stack([out_modes, back_modes])[None]
    piece = lax.all_gather(outgoing, "gx", axis=0, tiled=True)
    first = jnp.einsum("kx,ifmks->ifmxs", cos_local, piece, preferred_element_type=jnp.float32)
    second = jnp.einsum("kx,ifmks->ifmxs", sin_local, piece, preferred_element_type=jnp.float32)
    spread = fold_inverse(first, second, channels).astype(jnp.bfloat16)
    shared = lax.all_gather(spread, "gy", axis=2, tiled=True)
    ordered = jnp.transpose(shared, (1, 0, 2, 3, 4)).reshape(2, modes, pair_count, x_cells, doubled)
    first = jnp.einsum("ky,fkpxs->fxyps", cos_y, ordered, preferred_element_type=jnp.float32)
    second = jnp.einsum("ky,fkpxs->fxyps", sin_y, ordered, preferred_element_type=jnp.float32)
    spatial = fold_inverse(first, second, channels)
    field5 = field.reshape(x_cells, y_cells, pair_count, 2, channels)
    cot5 = cotangent.reshape(x_cells, y_cells, pair_count, 2, channels)
    direct = jnp.einsum("xyprc,cd->xyprd", field5, mix_weight, preferred_element_type=jnp.float32)
    mixed = (direct.reshape(x_cells, y_cells, pair_count, doubled) + spatial[0]).astype(
        jnp.bfloat16
    )
    direct_back = jnp.einsum(
        "xyprd,cd->xyprc", cot5, mix_weight, preferred_element_type=jnp.float32
    )
    field_grad = (direct_back.reshape(x_cells, y_cells, pair_count, doubled) + spatial[1]).astype(
        jnp.bfloat16
    )
    local_grad = jnp.einsum("xyprc,xyprd->cd", field5, cot5, preferred_element_type=jnp.float32)
    local_grad = local_grad / math.sqrt(2 * total_x * total_y * pair_count)
    mix_grad = lax.psum(local_grad, ("gx", "gy"))
    return (mixed, field_grad, spectral_grad, mix_grad)


def solution(mesh):
    placed = (
        P(("groups", "gx"), "gy", None, None),
        P(("groups", "gx"), "gy", None, None),
        P(None, ("gx", "gy"), None, None),
        P(),
    )
    return jax.shard_map(
        on_device,
        mesh=mesh,
        in_specs=placed,
        out_specs=(
            P(("groups", "gx"), "gy", None, None),
            P(("groups", "gx"), "gy", None, None),
            P("groups", ("gx", "gy"), None, None),
            P("groups", None),
        ),
        check_vma=False,
    )
```

profile of v0, /device:TPU:0, one launch (start us, length us, event | category | flops | bytes accessed | tf_op | source)
XLA Modules:
  0.0 486.0 jit_solution(14255243888477261410)
XLA Ops:
  7.2 0.0 copy-start
  7.2 0.0 reduce-scatter.5.cloned.1.call-start
  7.2 12.4 %copy.63 = bf16[32,128,8,128]{1,3,2,0:T(8,128)(2,1)} copy(bf16[32,128,8,128]{3,2,1,0:T(8,128)(2,1)} %param.5) | data formatting | bytes 16777216 | tf_op args[1]
  19.7 9.7 %convolution_bitcast_fusion.4 = f32[24,8,32,128]{3,0,1,2:T(8,128)} fusion(bf16[32,128,8,128]{1,3,2,0:T(8,128)(2,1)} %copy.63, s32[128]{0:T(128)S(1)} %iota_add_fusion.1, s32[24]{0:T(128)S(1)} %compare_select_fusion), kind=kOutput, calls=%fused_computation.47 | convolution fusion | flops 201375744 | bytes 11534944 | tf_op jit(solution)/shard_map/ky,xyps->kpxs/dot_general | solution.py:47
  29.4 0.0 copy-done.3
  29.4 6.2 %convolution_bitcast_fusion.5 = f32[24,8,32,128]{3,0,1,2:T(8,128)} fusion(bf16[32,128,8,128]{1,3,2,0:T(8,128)(2,1)S(1)} %copy-done.3, s32[128]{0:T(128)S(1)} %iota_add_fusion.1, s32[24]{0:T(128)S(1)} %compare_select_fusion), kind=kOutput, calls=%fused_computation.48 | convolution fusion | flops 201375744 | bytes 11534944 | tf_op jit(solution)/shard_map/ky,xyps->kpxs/dot_general | solution.py:46
  35.6 12.6 %copy.49 = bf16[32,128,8,128]{1,3,2,0:T(8,128)(2,1)} copy(bf16[32,128,8,128]{3,2,1,0:T(8,128)(2,1)} %param.4) | data formatting | bytes 16777216 | tf_op args[0]
  48.2 0.0 copy-start.2
  48.2 8.0 %convolution_bitcast_fusion.6 = f32[24,8,32,128]{3,0,1,2:T(8,128)S(1)} fusion(bf16[32,128,8,128]{1,3,2,0:T(8,128)(2,1)} %copy.49, s32[128]{0:T(128)S(1)} %iota_add_fusion.1, s32[24]{0:T(128)S(1)} %compare_select_fusion), kind=kOutput, calls=%fused_computation.49 | convolution fusion | flops 201375744 | bytes 11534944 | tf_op jit(solution)/shard_map/ky,xyps->kpxs/dot_general | solution.py:47
  56.3 0.0 copy-done.2
  56.3 6.2 %convolution_bitcast_fusion.7 = f32[24,8,32,128]{3,0,1,2:T(8,128)} fusion(bf16[32,128,8,128]{1,3,2,0:T(8,128)(2,1)S(1)} %copy-done.2, s32[128]{0:T(128)S(1)} %iota_add_fusion.1, s32[24]{0:T(128)S(1)} %compare_select_fusion), kind=kOutput, calls=%fused_computation.50 | convolution fusion | flops 201375744 | bytes 11534944 | tf_op jit(solution)/shard_map/ky,xyps->kpxs/dot_general | solution.py:46
  62.5 6.4 %slice_add_fusion.2 = (f32[24,8,32,64]{3,0,1,2:T(8,128)S(1)}, f32[24,8,32,64]{3,0,1,2:T(8,128)S(1)}) fusion(f32[24,8,32,128]{3,0,1,2:T(8,128)} %convolution_bitcast_fusion.4, f32[24,8,32,128]{3,0,1,2:T(8,128)} %convolution_bitcast_fusion.5), kind=kLoop, calls=%fused_computation.26 | loop fusion | flops 786432 | bytes 9437184 | tf_op jit(solution)/shard_map/add | solution.py:23
  68.9 0.9 pad_maximum_fusion.4
  69.8 0.0 copy-start.5
  69.8 1.8 copy.56
  71.6 0.1 copy-done.5
  71.7 1.7 slice_add_fusion.3
  73.4 0.9 pad_maximum_fusion.3
  74.2 2.3 copy.53
  76.5 3.4 pad_maximum_fusion.2
  79.9 20.7 %all-reduce.2 = bf16[8,2,24,32,128]{4,3,2,0,1:T(8,128)(2,1)S(1)} all-reduce(f32[8,2,24,32,128]{4,3,2,0,1:T(8,128)} %pad_maximum_fusion.2), channel_id=3, replica_groups=mesh['groups'=2,'gx'=8,'gy'=2] {'gy'}, use_global_device_ids=true, to_apply=%region_0.1.clone | all-reduce | flops 1572864 | bytes 9437184
  100.7 0.6 dynamic-slice
  101.9 0.6 convolution_bitcast_fusion.8
  102.5 0.6 convolution_bitcast_fusion.9
  103.1 1.3 slice_add_fusion.4
  104.4 2.1 pad_maximum_fusion.5
  106.5 0.0 reduce-scatter.5.cloned.1.call-update
  106.5 0.0 all-gather.6.cloned.1.call-start
  106.5 71.6 %reduce-scatter.5.cloned.1.call-done = f32[1,2,12,24,128]{4,3,2,1,0:T(8,128)} async-done(((f32[8,2,12,24,128]{4,3,2,1,0:T(8,128)}), f32[1,2,12,24,128]{4,3,2,1,0:T(8,128)}) %reduce-scatter.5.cloned.1.call-update) | async-done | bytes 294928 | tf_op jit(solution)/shard_map/reduce_scatter | solution.py:57
  178.1 1.0 convert_element_type.54
  179.2 0.1 convert_bitcast_fusion.2
  179.3 0.1 maximum_bitcast_fusion
  179.4 0.0 slice-start
  179.4 5.0 %fusion.12 = f32[12,24,1,64]{3,2,1,0:T(1,128)S(1)} fusion(bf16[24,12,64,128]{3,2,1,0:T(8,128)(2,1)} %param.6, bf16[12,24,128,1]{2,1,0,3:T(8,128)(2,1)S(1)} %maximum_bitcast_fusion), kind=kOutput, calls=%fused_computation.32 | convolution fusion | flops 4718592 | bytes 4866048 | tf_op jit(solution)/shard_map/lks,klcs->lkc/dot_general | solution.py:83
  184.4 0.0 slice-start.1
  184.5 4.9 %fusion.14 = f32[12,24,1,64]{3,2,1,0:T(1,128)S(1)} fusion(bf16[24,12,64,128]{3,2,1,0:T(8,128)(2,1)} %param.6, bf16[12,24,128,1]{2,1,0,3:T(8,128)(2,1)S(1)} %get-tuple-element.33), kind=kOutput, calls=%fused_computation.34 | convolution fusion | flops 4718592 | bytes 4866048 | tf_op jit(solution)/shard_map/lks,klcs->lkc/dot_general | solution.py:80
  189.4 3.7 fusion.16
  193.1 0.0 slice-done
  193.1 1.3 fusion.18
  194.4 0.1 fusion.40
  194.6 0.8 maximum_maximum_fusion
  195.4 0.0 all-gather.6.cloned.1.call-update
  195.4 0.0 all-gather.4.cloned.1.call-start
  195.4 40.2 %all-gather.6.cloned.1.call-done = bf16[16,12,24,128]{3,2,1,0:T(8,128)(2,1)} async-done(((bf16[2,12,24,128]{3,2,1,0:T(8,128)(2,1)}), bf16[16,12,24,128]{3,2,1,0:T(8,128)(2,1)}) %all-gather.6.cloned.1.call-update) | async-done | bytes 1179664 | tf_op jit(solution)/shard_map/all_gather | solution.py:99
  235.6 2.1 convolution_bitcast_fusion.2
  237.7 0.7 convolution_bitcast_fusion.3
  238.5 1.7 fusion.11
  240.2 2.0 pad_maximum_fusion.6
  242.2 0.0 all-gather.4.cloned.1.call-update
  242.3 8.5 %fusion.29 = f32[64,64]{1,0:T(8,128)S(1)} fusion(bf16[32,128,8,2,64]{1,4,3,2,0:T(8,128)(2,1)} %bitcast.151, bf16[32,128,8,2,64]{1,4,3,2,0:T(8,128)(2,1)} %bitcast.149), kind=kOutput, calls=%fused_computation.57 | convolution fusion | flops 536875008 | bytes 16793600 | tf_op jit(solution)/shard_map/xyprc,xyprd->cd/dot_general | solution.py:120
  250.7 12.4 %copy.94 = bf16[32,128,8,128]{1,3,0,2:T(8,128)(2,1)} copy(bf16[32,128,8,128]{3,2,1,0:T(8,128)(2,1)} %param.5) | data formatting | bytes 16777216 | tf_op jit(solution)/shard_map/reshape | solution.py:109
  263.1 58.6 %psum.7 = f32[64,64]{1,0:T(8,128)} all-reduce(f32[64,64]{1,0:T(8,128)S(1)} %fusion.29), channel_id=1, replica_groups=mesh['groups'=2,'gx'=8,'gy'=2] {'gx','gy'}, use_global_device_ids=true, to_apply=%region_2.3 | all-reduce | flops 4096 | bytes 32768 | tf_op jit(solution)/shard_map/psum | solution.py:122
  321.7 11.7 %fusion.44 = f32[32,128,8,2,64]{1,4,3,2,0:T(8,128)} fusion(bf16[32,128,8,2,64]{1,4,3,2,0:T(8,128)(2,1)} %bitcast.150, bf16[64,64]{1,0:T(8,128)(2,1)S(1)} %copy-done), kind=kOutput, calls=%fused_computation.94 | convolution fusion | flops 536870912 | bytes 25174016 | tf_op jit(solution)/shard_map/xyprc,cd->xyprd/dot_general | solution.py:110
  333.4 0.0 copy-done.4
  333.4 8.1 %fusion.42 = f32[32,128,8,2,64]{1,4,3,0,2:T(8,128)} fusion(bf16[32,128,8,2,64]{1,4,3,0,2:T(8,128)(2,1)S(1)} %bitcast.154, bf16[64,64]{1,0:T(8,128)(2,1)S(1)} %copy-done), kind=kOutput, calls=%fused_computation.92 | convolution fusion | flops 536870912 | bytes 25174016 | tf_op jit(solution)/shard_map/xyprd,cd->xyprc/dot_general | solution.py:114
  341.7 7.1 %multiply_add_fusion = (f32[24,12,64,64]{3,2,1,0:T(8,128)}, f32[24,12,64,64]{3,2,1,0:T(8,128)}) fusion(f32[24,12,64]{2,1,0:T(8,128)S(1)} %copy.68, f32[24,12,64]{2,1,0:T(8,128)S(1)} %copy.67, f32[24,12,64]{2,1,0:T(8,128)S(1)} %copy.66, f32[24,12,64]{2,1,0:T(8,128)S(1)} %copy.65), kind=kLoop, calls=%fused_computation.16 | loop fusion | flops 7077888 | bytes 9732096 | tf_op jit(solution)/shard_map/add | solution.py:91
  348.8 13.4 %pad_maximum_fusion.1 = f32[24,12,64,128]{3,2,1,0:T(8,128)} fusion(f32[24,12,64,64]{3,2,1,0:T(8,128)} %get-tuple-element.29, f32[24,12,64,64]{3,2,1,0:T(8,128)} %get-tuple-element.28), kind=kLoop, calls=%fused_computation.14 | loop fusion | flops 2359296 | bytes 18874368 | tf_op jit(solution)/shard_map/concatenate | solution.py:97
  362.3 2.4 copy.59
  364.7 13.3 %convolution_bitcast_fusion = f32[2,32,128,8,128]{2,4,1,3,0:T(8,128)} fusion(bf16[2,24,8,32,128]{4,3,2,1,0:T(8,128)(2,1)S(1)} %bitcast.152, s32[128]{0:T(128)S(1)} %iota_add_fusion.1, s32[24]{0:T(128)S(1)} %compare_select_fusion), kind=kOutput, calls=%fused_computation.2 | convolution fusion | flops 402702336 | bytes 36700768 | tf_op jit(solution)/shard_map/ky,fkpxs->fxyps/dot_general | solution.py:106
  378.0 13.5 %convolution_bitcast_fusion.1 = f32[2,32,128,8,128]{2,4,1,3,0:T(8,128)} fusion(bf16[2,24,8,32,128]{4,3,2,1,0:T(8,128)(2,1)S(1)} %bitcast.153, s32[128]{0:T(128)S(1)} %iota_add_fusion.1, s32[24]{0:T(128)S(1)} %compare_select_fusion), kind=kOutput, calls=%fused_computation.3 | convolution fusion | flops 402702336 | bytes 36700768 | tf_op jit(solution)/shard_map/ky,fkpxs->fxyps/dot_general | solution.py:105
  391.4 34.1 %slice_add_fusion = (f32[2,32,128,8,64]{2,4,1,3,0:T(8,128)}, f32[2,32,128,8,64]{2,4,1,3,0:T(8,128)}) fusion(f32[2,32,128,8,128]{2,4,1,3,0:T(8,128)} %convolution_bitcast_fusion, f32[2,32,128,8,128]{2,4,1,3,0:T(8,128)} %convolution_bitcast_fusion.1), kind=kLoop, calls=%fused_computation.12 | loop fusion | flops 8388608 | bytes 100663296 | tf_op jit(solution)/shard_map/add | solution.py:30
  425.5 28.8 %fusion.6 = (bf16[32,128,8,128]{1,3,0,2:T(8,128)(2,1)}, bf16[32,128,8,128]{1,3,0,2:T(8,128)(2,1)}) fusion(f32[2,32,128,8,64]{2,4,1,3,0:T(8,128)} %get-tuple-element.16, f32[2,32,128,8,64]{2,4,1,3,0:T(8,128)} %get-tuple-element.17, f32[32,128,8,2,64]{1,4,3,0,2:T(8,128)} %fusion.42, f32[32,128,8,2,64]{1,4,3,2,0:T(8,128)} %fusion.44), kind=kLoop, calls=%fused_computation.11 | loop fusion | flops 25165824 | bytes 83886080 | tf_op jit(solution)/shard_map/convert_element_type | solution.py:117
  454.4 12.4 %copy.71 = bf16[32,128,8,128]{3,2,1,0:T(8,128)(2,1)} copy(bf16[32,128,8,128]{1,3,0,2:T(8,128)(2,1)} %get-tuple-element.19) | data formatting | bytes 16777216
  466.8 12.4 %copy.72 = bf16[32,128,8,128]{3,2,1,0:T(8,128)(2,1)} copy(bf16[32,128,8,128]{1,3,0,2:T(8,128)(2,1)} %get-tuple-element.18) | data formatting | bytes 16777216
  (22 shorter events, 0.3 us)
Async XLA Ops:
  7.2 314.5 %copy-start = (bf16[64,64]{1,0:T(8,128)(2,1)S(1)}, bf16[64,64]{1,0:T(8,128)(2,1)}, u32[]{:S(2)}) copy-start(bf16[64,64]{1,0:T(8,128)(2,1)} %param.7) | copy-start | bytes 24580
  7.2 171.0 %reduce-scatter.5.cloned.1.call-start = ((), (), s32[]{:S(2)}) async-start(), calls=%async_computation.1 | async-start | bytes 2654208 | tf_op jit(solution)/shard_map/reduce_scatter | solution.py:57
  19.7 9.7 %copy-start.3 = (bf16[32,128,8,128]{1,3,2,0:T(8,128)(2,1)S(1)}, bf16[32,128,8,128]{1,3,2,0:T(8,128)(2,1)}, u32[]{:S(2)}) copy-start(bf16[32,128,8,128]{1,3,2,0:T(8,128)(2,1)} %copy.63) | copy-start | bytes 25165828
  48.2 8.1 %copy-start.2 = (bf16[32,128,8,128]{1,3,2,0:T(8,128)(2,1)S(1)}, bf16[32,128,8,128]{1,3,2,0:T(8,128)(2,1)}, u32[]{:S(2)}) copy-start(bf16[32,128,8,128]{1,3,2,0:T(8,128)(2,1)} %copy.49) | copy-start | bytes 25165828
  69.8 1.9 copy-start.5
  79.9 20.7 %copy-start.7 = (u32[32]{0:T(128)S(1)}, u32[32]{0:T(128)}, u32[]{:S(2)}) copy-start(u32[32]{0:T(128)} %constant.52) | copy-start | bytes 388
  106.5 129.1 %all-gather.6.cloned.1.call-start = ((), (), s32[]{:S(2)}) async-start(), calls=%async_computation.3 | async-start | bytes 1327104 | tf_op jit(solution)/shard_map/all_gather | solution.py:99
  179.4 13.7 %slice-start = ((s8[4718592]{0:T(1024)(128)(4,1)}), s8[4194304]{0:T(1024)(128)(4,1)S(1)}, s32[]{:S(2)}) async-start(s8[4718592]{0:T(1024)(128)(4,1)} %bitcast.164), calls=%async_computation.4 | async-start | bytes 8388608
  184.4 8.6 %slice-start.1 = ((s8[4718592]{0:T(1024)(128)(4,1)}), s8[524288]{0:T(1024)(128)(4,1)S(1)}, s32[]{:S(2)}) async-start(s8[4718592]{0:T(1024)(128)(4,1)} %bitcast.164), calls=%async_computation.5 | async-start | bytes 1048576
  195.4 166.9 %all-gather.4.cloned.1.call-start = ((), (), s32[]{:S(2)}) async-start(), calls=%async_computation.2 | async-start | bytes 4718592 | tf_op jit(solution)/shard_map/all_gather | solution.py:103
  235.6 2.1 copy-start.6
  321.7 11.7 %copy-start.4 = (bf16[32,128,8,128]{1,3,0,2:T(8,128)(2,1)S(1)}, bf16[32,128,8,128]{1,3,0,2:T(8,128)(2,1)}, u32[]{:S(2)}) copy-start(bf16[32,128,8,128]{1,3,0,2:T(8,128)(2,1)} %copy.94) | copy-start | bytes 25165828
  466.8 12.4 %copy-start.1 = (bf16[64,64]{1,0:T(8,128)(2,1)S(1)}, bf16[64,64]{1,0:T(8,128)(2,1)}, u32[]{:S(2)}) copy-start(bf16[64,64]{1,0:T(8,128)(2,1)} %param.7) | copy-start | bytes 24580
Sparse Core Ops, SparseCore 0:
  106.6 71.4 reduce-scatter.4
  195.5 40.0 all-gather.5
  242.4 10.8 all-gather.3
where the time goes:
time: 491 us; the launch traced here: 486 us
  waiting for transfers between devices  112 us (23%)
  other arithmetic  106 us (22%)
  matrix products  104 us (21%)
  blocking collectives  79.3 us (16%)
  local copies, waits for them, and re-layouts  69.7 us (14%)
  between operations  14.9 us (3%)
    reduce_scatter x1, waiting for transfers between devices, on_device(): lax.psum_scatter(fold_forward(first, second, channels), 'gx', scatter_dim...  71.6 us
    psum x1, blocking collectives, on_device(): mix_grad = lax.psum(local_grad, ('gx', 'gy'))  58.6 us
    unnamed x25, local copies, waits for them, and re-layouts  50.6 us
    all_gather x1, waiting for transfers between devices, on_device(): piece = lax.all_gather(outgoing, 'gx', axis=0, tiled=True)  40.2 us
    add x1, other arithmetic, fold_inverse(): imag = first[..., half:] + second[..., :half]  34.1 us
    convert_element_type x1, other arithmetic, on_device(): (direct_back.reshape(x_cells, y_cells, pair_count, doubled) + spatial[1])...  28.8 us
    unnamed x1, blocking collectives  20.7 us
    dot_general x2, matrix products, transform_rows(): jnp.einsum('ky,xyps->kpxs', sin_y, data, preferred_element_type=jnp.float32)  17.8 us
  transfers between devices with their start and end apart: 3, of which 2 were waited for; matrix products, arithmetic and copies ran while one was open for 13% of the time, Pallas kernels for 0%

commit v1 on v0

v1 whole, which is shorter than its diff:
```python
import functools
import math

import jax
import jax.numpy as jnp
import ml_dtypes
import numpy as np
from jax import lax
from jax.experimental import pallas as pl
from jax.experimental.pallas import tpu as pltpu
from jax.sharding import PartitionSpec as P

VMEM_LIMIT = 48 * 1024 * 1024
SLOTS = 32


def wave_tables(length, freqs):
    places = np.arange(length, dtype=np.int64)
    phase = (freqs[:, None] * places[None, :]) % length
    angle = phase.astype(np.float32) * np.float32(2.0 * math.pi / length)
    factor = np.float32(1.0 / math.sqrt(length))
    cos = (np.cos(angle) * factor).astype(ml_dtypes.bfloat16).astype(np.float32)
    sin = (np.sin(angle) * factor).astype(ml_dtypes.bfloat16).astype(np.float32)
    return cos, sin


def split_blocks(table, parts):
    shaped = table.reshape(table.shape[:-1] + (parts, -1))
    return np.moveaxis(shaped, -2, 0)


def make_tables(total_x, total_y, modes, pairs, nx, ny):
    half = modes // 2
    eye = np.eye(pairs, dtype=np.float32)
    cos, sin = wave_tables(total_y, np.arange(half + 1))
    slots = np.zeros((SLOTS, total_y), np.float32)
    slots[: half + 1] = cos
    slots[half + 1 : 2 * half + 1] = sin[1:]
    slots = split_blocks(slots, ny)
    y_fwd = np.einsum("bkn,pr->bkpnr", slots, eye)
    y_fwd = y_fwd[:, : 2 * half + 2].reshape(ny, (2 * half + 2) * pairs, -1)
    y_inv = np.einsum("bkn,pr->bnpkr", slots, eye).reshape(ny, -1, SLOTS * pairs)
    index = np.arange(modes)
    freqs = np.where(index < half, index, index - modes)
    cos, sin = wave_tables(total_x, freqs)
    both = split_blocks(np.stack([cos, sin]), nx)
    x_fwd = np.einsum("btqn,pr->btpqnr", both, eye).reshape(nx, 2 * pairs * modes, -1)
    x_inv = np.einsum("btqn,pr->btnprq", both, eye).reshape(nx, -1, pairs * modes)
    return [t.astype(ml_dtypes.bfloat16) for t in (y_fwd, y_inv, x_fwd, x_inv)]


def times_i(value, half):
    lane = lax.broadcasted_iota(jnp.int32, value.shape, 1)
    parts = [
        pltpu.roll(value[:, a : a + 2 * half], half, 1)
        for a in range(0, value.shape[1], 2 * half)
    ]
    swapped = jnp.concatenate(parts, axis=1) if len(parts) > 1 else parts[0]
    return jnp.where(lane % (2 * half) < half, -swapped, swapped)


def forward_kernel(modes, f_ref, c_ref, ty_ref, tx_ref, p_ref, g_ref, rows, total):
    step = pl.program_id(0)
    block, _, doubled = f_ref.shape
    half, pairs = modes // 2, rows.shape[2]
    channels = doubled // 2

    @pl.when(step == 0)
    def _():
        total[...] = jnp.zeros_like(total)

    def one(i, carry):
        f, c = f_ref[i], c_ref[i]
        both = jnp.concatenate([f, c], axis=1)
        t = jnp.dot(ty_ref[...], both, preferred_element_type=jnp.float32)
        cut = (half + 1) * pairs
        cos = t[:cut]
        sin = times_i(t[cut : cut + half * pairs], channels)
        at = step * block + i
        rows[at, 0] = cos[:pairs]
        for m in range(1, half + 1):
            even = cos[m * pairs : (m + 1) * pairs]
            odd = sin[(m - 1) * pairs : m * pairs]
            if m < half:
                rows[at, m] = even - odd
            rows[at, modes - m] = even + odd
        total[...] += lax.dot_general(
            f, c, (((0,), (0,)), ((), ())), preferred_element_type=jnp.float32
        )
        return carry

    lax.fori_loop(0, block, one, 0)

    @pl.when(step == pl.num_programs(0) - 1)
    def _():
        def mode(k, carry):
            data = rows[:, k].reshape(-1, 2 * doubled).astype(jnp.bfloat16)
            t = jnp.dot(tx_ref[...], data, preferred_element_type=jnp.float32)
            n = pairs * modes
            hat = t[:n] - times_i(t[n:], channels)
            p_ref[pl.ds(k * pairs, pairs)] = hat.reshape(pairs, modes, 2 * doubled).astype(
                jnp.bfloat16
            )
            return carry

        lax.fori_loop(0, modes, mode, 0)
        g_ref[...] = total[:channels, :channels] + total[channels:, channels:]


def barrier_with(n, me, core):
    barrier = pltpu.get_barrier_semaphore()
    pl.semaphore_signal(barrier, inc=1, device_id={"gy": 1 - core})

    def greet(s, carry):
        pl.semaphore_signal(barrier, inc=1, device_id={"gx": lax.rem(me + s, n)})
        return carry

    lax.fori_loop(1, n, greet, 0)
    pl.semaphore_wait(barrier, n)


def reduce_kernel(
    n, scale, p_ref, g_ref, hat_ref, mix_ref, got, mine, parts, g_got, g_all,
    send1, recv1, send2, recv2, g_send, g_recv, g_send2, g_recv2,
):
    me, core = lax.axis_index("gx"), lax.axis_index("gy")
    barrier_with(n, me, core)

    def to_core(j):
        return pltpu.make_async_remote_copy(
            src_ref=p_ref.at[j, 1 - core], dst_ref=got.at[j],
            send_sem=send1.at[j], recv_sem=recv1.at[j], device_id={"gy": 1 - core},
        )

    def to_owner(j, slot):
        return pltpu.make_async_remote_copy(
            src_ref=mine.at[j], dst_ref=parts.at[slot],
            send_sem=send2.at[j], recv_sem=recv2.at[slot], device_id={"gx": j},
        )

    def g_to(j, slot):
        return pltpu.make_async_remote_copy(
            src_ref=g_all.at[me], dst_ref=g_all.at[slot],
            send_sem=g_send2.at[j], recv_sem=g_recv2.at[slot], device_id={"gx": j},
        )

    g_core = pltpu.make_async_remote_copy(
        src_ref=g_ref, dst_ref=g_got, send_sem=g_send, recv_sem=g_recv,
        device_id={"gy": 1 - core},
    )

    def start_core(s, carry):
        to_core(lax.rem(me + s, n)).start()
        return carry

    lax.fori_loop(1, n + 1, start_core, 0)
    g_core.start()

    def combine(s, carry):
        j = lax.rem(me + s, n)
        to_core(j).wait_recv()
        mine[j] = (
            p_ref[j, core].astype(jnp.float32) + got[j].astype(jnp.float32)
        ).astype(jnp.bfloat16)

        @pl.when(s < n)
        def _():
            to_owner(j, me).start()

        return carry

    lax.fori_loop(1, n + 1, combine, 0)
    g_core.wait_recv()
    g_all[me] = g_ref[...] + g_got[...]

    def start_g(s, carry):
        g_to(lax.rem(me + s, n), me).start()
        return carry

    lax.fori_loop(1, n, start_g, 0)
    hat_ref[...] = mine[me].astype(jnp.float32)

    def collect(s, carry):
        j = lax.rem(me + n - s, n)
        to_owner(j, j).wait_recv()
        hat_ref[...] += parts[j].astype(jnp.float32)
        g_to(j, j).wait_recv()
        return carry

    lax.fori_loop(1, n, collect, 0)
    mix = g_all[0]
    for j in range(1, n):
        mix = mix + g_all[j]
    mix_ref[...] = mix * scale

    def drain(s, carry):
        j = lax.rem(me + s, n)
        to_core(j).wait_send()

        @pl.when(s < n)
        def _():
            to_owner(j, me).wait_send()
            g_to(j, me).wait_send()

        return carry

    lax.fori_loop(1, n + 1, drain, 0)
    g_core.wait_send()


def gather_kernel(n, z_ref, all_ref, send1, recv1, send2, recv2):
    me, core = lax.axis_index("gx"), lax.axis_index("gy")
    barrier_with(n, me, core)
    all_ref[me, core] = z_ref[...]

    def to_peer(j, slot):
        return pltpu.make_async_remote_copy(
            src_ref=all_ref.at[me, core], dst_ref=all_ref.at[slot, core],
            send_sem=send1.at[j], recv_sem=recv1.at[slot], device_id={"gx": j},
        )

    def to_core(j, side):
        return pltpu.make_async_remote_copy(
            src_ref=all_ref.at[j, side], dst_ref=all_ref.at[j, side],
            send_sem=send2.at[j], recv_sem=recv2.at[j], device_id={"gy": 1 - core},
        )

    def start(s, carry):
        to_peer(lax.rem(me + s, n), me).start()
        return carry

    lax.fori_loop(1, n, start, 0)
    to_core(me, core).start()

    def forward(s, carry):
        j = lax.rem(me + n - s, n)
        to_peer(j, j).wait_recv()
        to_core(j, core).start()
        return carry

    lax.fori_loop(1, n, forward, 0)

    def finish(s, carry):
        j = lax.rem(me + n - s, n)
        to_core(j, 1 - core).wait_recv()
        to_core(j, core).wait_send()
        return carry

    lax.fori_loop(0, n, finish, 0)

    def drain(s, carry):
        to_peer(lax.rem(me + s, n), me).wait_send()
        return carry

    lax.fori_loop(1, n, drain, 0)


def modes_kernel(hat_ref, turned_ref, w_ref, z_ref, grad_ref):
    block, count, channels, doubled = w_ref.shape
    rows = lax.broadcasted_iota(jnp.int32, (8, doubled), 0)

    def one(i, carry):
        for g in range(count):
            cot = hat_ref[i, g : g + 1, doubled:]
            turned = -times_i(cot, channels)
            real = turned_ref[i, :channels, g : g + 1]
            imag = turned_ref[i, channels:doubled, g : g + 1]
            weight16 = w_ref[i, g]
            weight = weight16.astype(jnp.float32)
            grad_ref[i, g] = real * cot + imag * turned
            first = jnp.sum(real * weight, axis=0, keepdims=True)
            second = jnp.sum(imag * weight, axis=0, keepdims=True)
            z_ref[i, g : g + 1, :doubled] = first + times_i(second, channels)
            sides = jnp.where(rows == 0, cot, turned).astype(jnp.bfloat16)
            back = lax.dot_general(
                sides, weight16, (((1,), (1,)), ((), ())), preferred_element_type=jnp.float32
            )
            z_ref[i, g : g + 1, doubled:] = jnp.concatenate([back[0:1], back[1:2]], axis=1)
        return carry

    lax.fori_loop(0, block, one, 0)


def inverse_kernel(modes, f_ref, c_ref, z_ref, ty_ref, tx_ref, mix_ref, o_ref, b_ref, spread):
    step = pl.program_id(0)
    block, _, doubled = f_ref.shape
    half, pairs = modes // 2, spread.shape[2]
    channels = doubled // 2
    cells = spread.shape[0]

    @pl.when(step == 0)
    def _():
        def expand(k):
            data = z_ref[pl.ds(k * pairs, pairs)].reshape(pairs * modes, 2 * doubled)
            t = jnp.dot(
                tx_ref[...], data.astype(jnp.bfloat16), preferred_element_type=jnp.float32
            )
            n = cells * pairs
            return t[:n] + times_i(t[n:], channels)

        def put(slot, value):
            spread[:, slot] = value.reshape(cells, pairs, 2 * doubled)

        put(0, expand(0))

        def pair(m, carry):
            plus, minus = expand(m), expand(modes - m)
            put(m, plus + minus)
            put(half + m, times_i(plus - minus, channels))
            return carry

        lax.fori_loop(1, half, pair, 0)
        last = expand(half)
        put(half, last)
        put(2 * half, -times_i(last, channels))
        spread[:, 2 * half + 1 :] = jnp.zeros_like(spread[:, 2 * half + 1 :])

    def one(i, carry):
        modes_here = spread[step * block + i].reshape(-1, 2 * doubled).astype(jnp.bfloat16)
        left = jnp.concatenate([ty_ref[...], f_ref[i], c_ref[i]], axis=1)
        right = jnp.concatenate([modes_here, mix_ref[...]], axis=0)
        out = jnp.dot(left, right, preferred_element_type=jnp.float32)
        o_ref[i] = out[:, :doubled].astype(jnp.bfloat16)
        b_ref[i] = out[:, doubled:].astype(jnp.bfloat16)
        return carry

    lax.fori_loop(0, block, one, 0)


def whole(shape):
    zeros = (0,) * len(shape)
    return pl.BlockSpec(shape, lambda i: zeros)


def on_device(field, cotangent, spectral_weight, mix_weight):
    x_cells, y_cells, pairs, doubled = field.shape
    channels = doubled // 2
    modes = spectral_weight.shape[0]
    count = spectral_weight.shape[1]
    nx, ny = lax.axis_size("gx"), lax.axis_size("gy")
    total_x, total_y = x_cells * nx, y_cells * ny
    me, core = lax.axis_index("gx"), lax.axis_index("gy")
    tables = make_tables(total_x, total_y, modes, pairs, nx, ny)
    ty_fwd, ty_inv, tx_fwd, tx_inv = [
        lax.dynamic_index_in_dim(jnp.asarray(t), at, 0, keepdims=False)
        for t, at in zip(tables, (core, core, me, me))
    ]
    flat = (x_cells, y_cells * pairs, doubled)
    field2, cot2 = field.reshape(flat), cotangent.reshape(flat)
    block = 4
    grid = (x_cells // block,)
    data_spec = pl.BlockSpec((block,) + flat[1:], lambda i: (i, 0, 0))
    wide = 2 * doubled
    groups = modes * pairs
    params = pltpu.CompilerParams(vmem_limit_bytes=VMEM_LIMIT)

    partial, grad_part = pl.pallas_call(
        functools.partial(forward_kernel, modes),
        grid=grid,
        out_shape=(
            jax.ShapeDtypeStruct((groups, modes, wide), jnp.bfloat16),
            jax.ShapeDtypeStruct((channels, channels), jnp.float32),
        ),
        in_specs=[data_spec, data_spec, whole(ty_fwd.shape), whole(tx_fwd.shape)],
        out_specs=(whole((groups, modes, wide)), whole((channels, channels))),
        scratch_shapes=[
            pltpu.VMEM((x_cells, modes, pairs, wide), jnp.float32),
            pltpu.VMEM((doubled, doubled), jnp.float32),
        ],
        compiler_params=params,
        name="forward",
    )(field2, cot2, ty_fwd, tx_fwd)

    vmem = pl.BlockSpec(memory_space=pltpu.VMEM)
    share = (count, modes, wide)
    dma = pltpu.SemaphoreType.DMA
    hat, mix_grad = pl.pallas_call(
        functools.partial(
            reduce_kernel, nx, 1.0 / math.sqrt(2 * total_x * total_y * pairs)
        ),
        out_shape=(
            jax.ShapeDtypeStruct(share, jnp.float32),
            jax.ShapeDtypeStruct((channels, channels), jnp.float32),
        ),
        in_specs=[vmem, vmem],
        out_specs=(vmem, vmem),
        scratch_shapes=[
            pltpu.VMEM((nx,) + share, jnp.bfloat16),
            pltpu.VMEM((nx,) + share, jnp.bfloat16),
            pltpu.VMEM((nx,) + share, jnp.bfloat16),
            pltpu.VMEM((channels, channels), jnp.float32),
            pltpu.VMEM((nx, channels, channels), jnp.float32),
            dma((nx,)), dma((nx,)), dma((nx,)), dma((nx,)),
            dma, dma, dma((nx,)), dma((nx,)),
        ],
        compiler_params=pltpu.CompilerParams(
            collective_id=0, has_side_effects=True, vmem_limit_bytes=VMEM_LIMIT
        ),
        name="reduce",
    )(partial.reshape((nx, ny) + share), grad_part)

    hat = jnp.transpose(hat, (1, 0, 2)).astype(jnp.bfloat16).astype(jnp.float32)
    turned = jnp.transpose(hat[:, :, :doubled], (0, 2, 1))
    qb = 4
    z, spectral_grad = pl.pallas_call(
        modes_kernel,
        grid=(modes // qb,),
        out_shape=(
            jax.ShapeDtypeStruct((modes, count, wide), jnp.float32),
            jax.ShapeDtypeStruct((modes, count, channels, doubled), jnp.float32),
        ),
        in_specs=[
            pl.BlockSpec((qb, count, wide), lambda i: (i, 0, 0)),
            pl.BlockSpec((qb, doubled, count), lambda i: (i, 0, 0)),
            pl.BlockSpec((qb, count, channels, doubled), lambda i: (i, 0, 0, 0)),
        ],
        out_specs=(
            pl.BlockSpec((qb, count, wide), lambda i: (i, 0, 0)),
            pl.BlockSpec((qb, count, channels, doubled), lambda i: (i, 0, 0, 0)),
        ),
        compiler_params=params,
        name="modes",
    )(hat, turned, spectral_weight)
    z = jnp.transpose(z, (1, 0, 2)).astype(jnp.bfloat16)

    everything = pl.pallas_call(
        functools.partial(gather_kernel, nx),
        out_shape=jax.ShapeDtypeStruct((nx, ny) + share, jnp.bfloat16),
        in_specs=[vmem],
        out_specs=vmem,
        scratch_shapes=[dma((nx,)), dma((nx,)), dma((nx,)), dma((nx,))],
        compiler_params=pltpu.CompilerParams(
            collective_id=1, has_side_effects=True, vmem_limit_bytes=VMEM_LIMIT
        ),
        name="gather",
    )(z)

    empty = jnp.zeros_like(mix_weight)
    back = mix_weight.T
    rows = [
        [mix_weight if a == b else empty for b in range(2)] + [empty] * 2 for a in range(2)
    ] + [[empty] * 2 + [back if a == b else empty for b in range(2)] for a in range(2)]
    mixing = jnp.block(rows)
    mixed, field_grad = pl.pallas_call(
        functools.partial(inverse_kernel, modes),
        grid=grid,
        out_shape=(jax.ShapeDtypeStruct(flat, jnp.bfloat16),) * 2,
        in_specs=[
            data_spec, data_spec, whole((groups, modes, wide)),
            whole(ty_inv.shape), whole(tx_inv.shape), whole(mixing.shape),
        ],
        out_specs=(data_spec, data_spec),
        scratch_shapes=[pltpu.VMEM((x_cells, SLOTS, pairs, wide), jnp.float32)],
        compiler_params=params,
        name="inverse",
    )(field2, cot2, everything.reshape(groups, modes, wide), ty_inv, tx_inv, mixing)
    return (
        mixed.reshape(field.shape), field_grad.reshape(field.shape), spectral_grad, mix_grad
    )


def solution(mesh):
    placed = (
        P(("groups", "gx"), "gy", None, None),
        P(("groups", "gx"), "gy", None, None),
        P(None, ("gx", "gy"), None, None),
        P(),
    )
    return jax.shard_map(
        on_device,
        mesh=mesh,
        in_specs=placed,
        out_specs=(
            P(("groups", "gx"), "gy", None, None),
            P(("groups", "gx"), "gy", None, None),
            P("groups", ("gx", "gy"), None, None),
            P("groups", None),
        ),
        check_vma=False,
    )
```

time: 491 us -> 151 us (0.31)
  the two profiles are of different devices: /device:TPU:0 before, /device:TPU:29 now
where the time goes in v1:
time: 151 us; the launch traced here: 150 us
  Pallas kernels  139 us (92%)
  local copies, waits for them, and re-layouts  9.49 us (6%)
    pallas_call x1, Pallas kernels, on_device(): pl.pallas_call(functools.partial(reduce_kernel, nx, 1.0 / math.sqrt(2 * t...  37.6 us
    pallas_call x1, Pallas kernels, on_device(): pl.pallas_call(functools.partial(gather_kernel, nx), out_shape=jax.ShapeD...  31.9 us
    pallas_call x1, Pallas kernels, on_device(): pl.pallas_call(functools.partial(inverse_kernel, modes), grid=grid, out_s...  25.1 us
    pallas_call x1, Pallas kernels, on_device(): pl.pallas_call(modes_kernel, grid=(modes // qb,), out_shape=(jax.ShapeDty...  22.6 us
    pallas_call x1, Pallas kernels, on_device(): pl.pallas_call(functools.partial(forward_kernel, modes), grid=grid, out_s...  22 us
    squeeze x4, local copies, waits for them, and re-layouts, on_device(): lax.dynamic_index_in_dim(jnp.asarray(t), at, 0, keepdims=False)  4.05 us

profile of v1, /device:TPU:29, one launch (start us, length us, event | category | flops | bytes accessed | tf_op | source)
XLA Modules:
  0.0 150.3 jit_solution(5296967685220388405)
XLA Ops:
  0.6 0.8 copy.15
  1.5 0.9 maximum_maximum_fusion.mix_ref
  2.4 0.9 dynamic-slice_bitcast_fusion.3.tx_ref
  3.3 1.0 dynamic-slice_bitcast_fusion.2.tx_ref
  4.3 1.0 dynamic-slice_bitcast_fusion.1.ty_ref
  5.4 1.1 dynamic-slice_bitcast_fusion.ty_ref
  6.4 22.0 %forward.1 = (bf16[192,24,256]{2,1,0:T(8,128)(2,1)S(1)}, f32[64,64]{1,0:T(8,128)S(1)}) custom-call(bf16[32,1024,128]{2,1,0:T(8,128)(2,1)} %bitcast.26, bf16[32,1024,128]{2,1,0:T(8,128)(2,1)} %bitcast.28, bf16[208,1024]{1,0:T(8,128)(2,1)S(1)} %dynamic-slice_bitcast_fusion.1.ty_ref, bf16[384,256]{1,0:T(8,128)(2,1)S(1)} %dynamic-slice_bitcast_fusion.3.tx_ref), custom_call_target="tpu_custom_call" | custom-call | tf_op jit(solution)/shard_map/forward/pallas_call | solution.py:357
  28.4 37.6 %reduce.1 = (f32[12,24,256]{2,1,0:T(8,128)S(1)}, f32[64,64]{1,0:T(8,128)S(1)}) custom-call(bf16[8,2,12,24,256]{4,3,2,1,0:T(8,128)(2,1)S(1)} %bitcast.24, f32[64,64]{1,0:T(8,128)S(1)} %get-tuple-element.13.g_ref), custom_call_target="tpu_custom_call" | custom-call | tf_op jit(solution)/shard_map/reduce/pallas_call | solution.py:377
  66.1 0.1 copy.13.hat_ref
  66.2 2.2 %copy.12 = f32[12,24,256]{0,2,1:T(8,128)} copy(f32[12,24,256]{2,1,0:T(8,128)S(1)} %get-tuple-element.20) | data formatting | bytes 589824 | tf_op jit(solution)/shard_map/convert_element_type | solution.py:402
  68.4 1.6 %slice_bitcast_fusion.turned_ref = f32[24,128,12]{2,1,0:T(8,128)S(1)} fusion(f32[24,12,256]{1,2,0:T(8,128)} %bitcast.30), kind=kLoop, calls=%fused_computation | loop fusion | bytes 294912 | tf_op jit(solution)/shard_map/transpose | solution.py:403
  70.0 22.6 %modes.1 = (f32[24,12,256]{2,1,0:T(8,128)S(1)}, f32[24,12,64,128]{3,2,1,0:T(8,128)}) custom-call(f32[24,12,256]{2,1,0:T(8,128)S(1)} %copy.13.hat_ref, f32[24,128,12]{2,1,0:T(8,128)S(1)} %slice_bitcast_fusion.turned_ref, bf16[24,12,64,128]{3,2,1,0:T(8,128)(2,1)} %w_ref.1), custom_call_target="tpu_custom_call" | custom-call | tf_op jit(solution)/shard_map/modes/pallas_call | solution.py:405
  92.6 0.2 copy.20
  92.7 31.9 %gather.1 = bf16[8,2,12,24,256]{4,3,2,1,0:T(8,128)(2,1)S(1)} custom-call(bf16[12,24,256]{2,1,0:T(8,128)(2,1)S(1)} %bitcast.25), custom_call_target="tpu_custom_call" | custom-call | tf_op jit(solution)/shard_map/gather/pallas_call | solution.py:426
  124.6 25.1 %inverse.1 = (bf16[32,1024,128]{2,1,0:T(8,128)(2,1)}, bf16[32,1024,128]{2,1,0:T(8,128)(2,1)}) custom-call(bf16[32,1024,128]{2,1,0:T(8,128)(2,1)} %bitcast.27, bf16[32,1024,128]{2,1,0:T(8,128)(2,1)} %bitcast.29, bf16[192,24,256]{2,1,0:T(8,128)(2,1)S(1)} %bitcast.23, bf16[1024,256]{1,0:T(8,128)(2,1)S(1)} %dynamic-slice_bitcast_fusion.ty_ref, ...), custom_call_target="tpu_custom_call" | custom-call | tf_op jit(solution)/shard_map/inverse/pallas_call | solution.py:444
  149.7 0.6 copy.22
  (2 shorter events, 0.0 us)

commit v2 on v1

v2 whole, which is shorter than its diff:
```python
import functools
import math

import jax
import jax.numpy as jnp
import ml_dtypes
import numpy as np
from jax import lax
from jax.experimental import pallas as pl
from jax.experimental.pallas import tpu as pltpu
from jax.sharding import PartitionSpec as P

VMEM_LIMIT = 48 * 1024 * 1024
SLOTS = 32


def wave_tables(length, freqs):
    places = np.arange(length, dtype=np.int64)
    phase = (freqs[:, None] * places[None, :]) % length
    angle = phase.astype(np.float32) * np.float32(2.0 * math.pi / length)
    factor = np.float32(1.0 / math.sqrt(length))
    cos = (np.cos(angle) * factor).astype(ml_dtypes.bfloat16).astype(np.float32)
    sin = (np.sin(angle) * factor).astype(ml_dtypes.bfloat16).astype(np.float32)
    return cos, sin


def split_blocks(table, parts):
    shaped = table.reshape(table.shape[:-1] + (parts, -1))
    return np.moveaxis(shaped, -2, 0)


def make_tables(total_x, total_y, modes, pairs, nx, ny):
    half = modes // 2
    eye = np.eye(pairs, dtype=np.float32)
    cos, sin = wave_tables(total_y, np.arange(half + 1))
    slots = np.zeros((SLOTS, total_y), np.float32)
    slots[: half + 1] = cos
    slots[half + 1 : 2 * half + 1] = sin[1:]
    slots = split_blocks(slots, ny)
    y_fwd = np.einsum("bkn,pr->bkpnr", slots, eye)
    y_fwd = y_fwd[:, : 2 * half + 2].reshape(ny, (2 * half + 2) * pairs, -1)
    y_inv = np.einsum("bkn,pr->bnpkr", slots, eye).reshape(ny, -1, SLOTS * pairs)
    index = np.arange(modes)
    freqs = np.where(index < half, index, index - modes)
    cos, sin = wave_tables(total_x, freqs)
    both = split_blocks(np.stack([cos, sin]), nx)
    x_fwd = np.einsum("btqn,pr->btpqnr", both, eye).reshape(nx, 2 * pairs * modes, -1)
    x_inv = np.einsum("btqn,pr->btnprq", both, eye).reshape(nx, -1, pairs * modes)
    return [t.astype(ml_dtypes.bfloat16) for t in (y_fwd, y_inv, x_fwd, x_inv)]


def times_i(value, half):
    lane = lax.broadcasted_iota(jnp.int32, value.shape, 1)
    parts = [
        pltpu.roll(value[:, a : a + 2 * half], half, 1)
        for a in range(0, value.shape[1], 2 * half)
    ]
    swapped = jnp.concatenate(parts, axis=1) if len(parts) > 1 else parts[0]
    return jnp.where(lane % (2 * half) < half, -swapped, swapped)


def forward_kernel(modes, _, f_ref, c_ref, ty_ref, tx_ref, p_ref, rows):
    step = pl.program_id(0)
    block, _, doubled = f_ref.shape
    half, pairs = modes // 2, rows.shape[2]
    channels = doubled // 2

    def one(i, carry):
        f, c = f_ref[i], c_ref[i]
        both = jnp.concatenate([f, c], axis=1)
        t = jnp.dot(ty_ref[0], both, preferred_element_type=jnp.float32)
        cut = (half + 1) * pairs
        cos = t[:cut]
        sin = times_i(t[cut : cut + half * pairs], channels)
        at = step * block + i
        rows[at, 0] = cos[:pairs]
        for m in range(1, half + 1):
            even = cos[m * pairs : (m + 1) * pairs]
            odd = sin[(m - 1) * pairs : m * pairs]
            if m < half:
                rows[at, m] = even - odd
            rows[at, modes - m] = even + odd
        return carry

    lax.fori_loop(0, block, one, 0)

    @pl.when(step == pl.num_programs(0) - 1)
    def _():
        def mode(k, carry):
            data = rows[:, k].reshape(-1, 2 * doubled).astype(jnp.bfloat16)
            t = jnp.dot(tx_ref[0], data, preferred_element_type=jnp.float32)
            n = pairs * modes
            hat = t[:n] - times_i(t[n:], channels)
            p_ref[pl.ds(k * pairs, pairs)] = hat.reshape(pairs, modes, 2 * doubled).astype(
                jnp.bfloat16
            )
            return carry

        lax.fori_loop(0, modes, mode, 0)


def barrier_with(n, me, core):
    hosts = n // 2
    high, low = me // 2, lax.rem(me, 2)
    barrier = pltpu.get_barrier_semaphore()
    pl.semaphore_signal(barrier, inc=1, device_id={"gy": 1 - core})
    pl.semaphore_signal(barrier, inc=1, device_id={"gx": high * 2 + 1 - low})

    def greet(s, carry):
        h = lax.rem(high + s, hosts)
        pl.semaphore_signal(barrier, inc=1, device_id={"gx": h * 2 + low})
        return carry

    lax.fori_loop(1, hosts, greet, 0)
    pl.semaphore_wait(barrier, hosts + 1)


def reduce_kernel(
    n, p_ref, f_hbm, c_hbm, hat_ref, g_ref, got, mine, side, parts, f_buf, c_buf, total,
    send1, recv1, send2, recv2, send3, recv3, f_sem, c_sem,
):
    me, core = lax.axis_index("gx"), lax.axis_index("gy")
    hosts = n // 2
    high, low = me // 2, lax.rem(me, 2)
    block = f_buf.shape[1]
    chunks = f_hbm.shape[0] // block
    channels = total.shape[0] // 2

    def fetch(i, slot):
        return (
            pltpu.make_async_copy(
                f_hbm.at[pl.ds(i * block, block)], f_buf.at[slot], f_sem.at[slot]
            ),
            pltpu.make_async_copy(
                c_hbm.at[pl.ds(i * block, block)], c_buf.at[slot], c_sem.at[slot]
            ),
        )

    for i in range(min(2, chunks)):
        for copy in fetch(i, i):
            copy.start()
    total[...] = jnp.zeros_like(total)
    barrier_with(n, me, core)

    def to_core(j):
        return pltpu.make_async_remote_copy(
            src_ref=p_ref.at[j, 1 - core], dst_ref=got.at[j],
            send_sem=send1.at[j], recv_sem=recv1.at[j], device_id={"gy": 1 - core},
        )

    def to_partner(h):
        return pltpu.make_async_remote_copy(
            src_ref=mine.at[h, 1], dst_ref=side.at[h],
            send_sem=send2.at[h], recv_sem=recv2.at[h], device_id={"gx": high * 2 + 1 - low},
        )

    def to_owner(h, slot):
        return pltpu.make_async_remote_copy(
            src_ref=mine.at[h, 0], dst_ref=parts.at[slot],
            send_sem=send3.at[h], recv_sem=recv3.at[slot], device_id={"gx": h * 2 + low},
        )

    def add_products(first, last):
        def one(i, carry):
            slot = lax.rem(i, 2)
            for copy in fetch(i, slot):
                copy.wait()
            for b in range(block):
                total[...] += lax.dot_general(
                    f_buf[slot, b], c_buf[slot, b], (((0,), (0,)), ((), ())),
                    preferred_element_type=jnp.float32,
                )

            @pl.when(i + 2 < chunks)
            def _():
                for copy in fetch(i + 2, slot):
                    copy.start()

            return carry

        lax.fori_loop(first, last, one, 0)

    def start_core(s, carry):
        h = lax.rem(high + s, hosts)
        to_core(h * 2 + 1 - low).start()
        return carry

    def start_core_own(s, carry):
        h = lax.rem(high + s, hosts)
        to_core(h * 2 + low).start()
        return carry

    lax.fori_loop(1, hosts + 1, start_core, 0)
    lax.fori_loop(1, hosts + 1, start_core_own, 0)

    def pass_on(s, carry):
        h = lax.rem(high + s, hosts)
        j = h * 2 + 1 - low
        to_core(j).wait_recv()
        mine[h, 1] = (
            p_ref[j, core].astype(jnp.float32) + got[j].astype(jnp.float32)
        ).astype(jnp.bfloat16)
        to_partner(h).start()
        return carry

    lax.fori_loop(1, hosts + 1, pass_on, 0)
    add_products(0, chunks // 4)

    def combine(s, carry):
        h = lax.rem(high + s, hosts)
        j = h * 2 + low
        to_core(j).wait_recv()
        to_partner(h).wait_recv()
        hat_ref[...] = (
            p_ref[j, core].astype(jnp.float32)
            + got[j].astype(jnp.float32)
            + side[h].astype(jnp.float32)
        )

        @pl.when(s < hosts)
        def _():
            mine[h, 0] = hat_ref[...].astype(jnp.bfloat16)
            to_owner(h, high).start()

        return carry

    lax.fori_loop(1, hosts + 1, combine, 0)
    add_products(chunks // 4, chunks)
    g_ref[...] = total[:channels, :channels] + total[channels:, channels:]

    def collect(s, carry):
        h = lax.rem(high + hosts - s, hosts)
        to_owner(h, h).wait_recv()
        hat_ref[...] += parts[h].astype(jnp.float32)
        return carry

    lax.fori_loop(1, hosts, collect, 0)

    def drain(s, carry):
        h = lax.rem(high + s, hosts)
        to_core(h * 2).wait_send()
        to_core(h * 2 + 1).wait_send()
        to_partner(h).wait_send()

        @pl.when(s < hosts)
        def _():
            to_owner(h, high).wait_send()

        return carry

    lax.fori_loop(1, hosts + 1, drain, 0)


def gather_kernel(
    n, scale, z_ref, g_ref, all_ref, mix_ref, g_core, g_pair, g_side, g_all,
    send_up, send_down, recv_z, send_y, recv_y, send_c, recv_c,
    g_send, g_recv, g_send2, g_recv2, g_send3, g_recv3,
):
    me, core = lax.axis_index("gx"), lax.axis_index("gy")
    hosts = n // 2
    high, low = me // 2, lax.rem(me, 2)
    partner = high * 2 + 1 - low
    barrier_with(n, me, core)
    all_ref[me, core] = z_ref[...]

    def along(h, step, sems):
        block = all_ref.at[h * 2 + low, core]
        return pltpu.make_async_remote_copy(
            src_ref=block, dst_ref=block, send_sem=sems.at[h], recv_sem=recv_z.at[h],
            device_id={"gx": me + 2 * step},
        )

    def to_partner(h, side):
        block = all_ref.at[h * 2 + side, core]
        return pltpu.make_async_remote_copy(
            src_ref=block, dst_ref=block, send_sem=send_y.at[h], recv_sem=recv_y.at[h],
            device_id={"gx": partner},
        )

    def to_core(j, side):
        block = all_ref.at[j, side]
        return pltpu.make_async_remote_copy(
            src_ref=block, dst_ref=block, send_sem=send_c.at[j], recv_sem=recv_c.at[j],
            device_id={"gy": 1 - core},
        )

    def g_to_core():
        return pltpu.make_async_remote_copy(
            src_ref=g_ref, dst_ref=g_core, send_sem=g_send, recv_sem=g_recv,
            device_id={"gy": 1 - core},
        )

    def g_to_partner():
        return pltpu.make_async_remote_copy(
            src_ref=g_pair, dst_ref=g_side, send_sem=g_send2, recv_sem=g_recv2,
            device_id={"gx": partner},
        )

    def g_to(h, slot):
        return pltpu.make_async_remote_copy(
            src_ref=g_all.at[high], dst_ref=g_all.at[slot],
            send_sem=g_send3.at[h], recv_sem=g_recv3.at[slot], device_id={"gx": h * 2 + low},
        )

    has_up, has_down = high < hosts - 1, high > 0

    @pl.when(has_up)
    def _():
        along(high, 1, send_up).start()

    @pl.when(has_down)
    def _():
        along(high, -1, send_down).start()

    to_partner(high, low).start()
    to_core(me, core).start()
    g_to_core().start()

    def from_partner(h):
        to_partner(h, 1 - low).wait_recv()
        to_core(h * 2 + 1 - low, core).start()

    for t in range(1, hosts):
        below, above = high - t, high + t

        @pl.when(below >= 0)
        def _():
            along(below, 1, send_up).wait_recv()

            @pl.when(has_up)
            def _():
                along(below, 1, send_up).start()

            to_partner(below, low).start()
            to_core(below * 2 + low, core).start()

        @pl.when(above < hosts)
        def _():
            along(above, -1, send_down).wait_recv()

            @pl.when(has_down)
            def _():
                along(above, -1, send_down).start()

            to_partner(above, low).start()
            to_core(above * 2 + low, core).start()

        if t == 1:
            from_partner(high)
            g_to_core().wait_recv()
            g_pair[...] = g_ref[...] + g_core[...]
            g_to_partner().start()

    g_to_partner().wait_recv()
    g_all[high] = g_pair[...] + g_side[...]

    def start_g(s, carry):
        g_to(lax.rem(high + s, hosts), high).start()
        return carry

    lax.fori_loop(1, hosts, start_g, 0)

    for t in range(1, hosts):
        below, above = high - t, high + t

        @pl.when(below >= 0)
        def _():
            from_partner(below)

        @pl.when(above < hosts)
        def _():
            from_partner(above)

    def finish(s, carry):
        h = lax.rem(high + s, hosts)
        for side in range(2):
            to_core(h * 2 + side, 1 - core).wait_recv()
            to_core(h * 2 + side, core).wait_send()
        to_partner(h, low).wait_send()

        @pl.when(has_up & (h <= high))
        def _():
            along(h, 1, send_up).wait_send()

        @pl.when(has_down & (h >= high))
        def _():
            along(h, -1, send_down).wait_send()

        @pl.when(s > 0)
        def _():
            g_to(h, h).wait_recv()
            g_to(h, high).wait_send()

        return carry

    lax.fori_loop(0, hosts, finish, 0)
    g_to_core().wait_send()
    g_to_partner().wait_send()
    mix = g_all[0]
    for h in range(1, hosts):
        mix = mix + g_all[h]
    mix_ref[...] = mix * scale


def modes_kernel(hat_ref, turned_ref, w_ref, z_ref, grad_ref):
    block, count, channels, doubled = w_ref.shape
    rows = lax.broadcasted_iota(jnp.int32, (8, doubled), 0)

    def one(i, carry):
        for g in range(count):
            cot = hat_ref[i, g : g + 1, doubled:]
            turned = -times_i(cot, channels)
            real = turned_ref[i, :channels, g : g + 1]
            imag = turned_ref[i, channels:doubled, g : g + 1]
            weight16 = w_ref[i, g]
            weight = weight16.astype(jnp.float32)
            grad_ref[i, g] = real * cot + imag * turned
            first = jnp.sum(real * weight, axis=0, keepdims=True)
            second = jnp.sum(imag * weight, axis=0, keepdims=True)
            z_ref[i, g : g + 1, :doubled] = first + times_i(second, channels)
            sides = jnp.where(rows == 0, cot, turned).astype(jnp.bfloat16)
            back = lax.dot_general(
                sides, weight16, (((1,), (1,)), ((), ())), preferred_element_type=jnp.float32
            )
            z_ref[i, g : g + 1, doubled:] = jnp.concatenate([back[0:1], back[1:2]], axis=1)
        return carry

    lax.fori_loop(0, block, one, 0)


def inverse_kernel(modes, _, f_ref, c_ref, z_ref, ty_ref, tx_ref, mix_ref, o_ref, b_ref, spread):
    step = pl.program_id(0)
    block, _, doubled = f_ref.shape
    half, pairs = modes // 2, spread.shape[2]
    channels = doubled // 2
    cells = spread.shape[0]

    @pl.when(step == 0)
    def _():
        def expand(k):
            data = z_ref[pl.ds(k * pairs, pairs)].reshape(pairs * modes, 2 * doubled)
            t = jnp.dot(
                tx_ref[0], data.astype(jnp.bfloat16), preferred_element_type=jnp.float32
            )
            n = cells * pairs
            return t[:n] + times_i(t[n:], channels)

        def put(slot, value):
            spread[:, slot] = value.reshape(cells, pairs, 2 * doubled)

        put(0, expand(0))

        def pair(m, carry):
            plus, minus = expand(m), expand(modes - m)
            put(m, plus + minus)
            put(half + m, times_i(plus - minus, channels))
            return carry

        lax.fori_loop(1, half, pair, 0)
        last = expand(half)
        put(half, last)
        put(2 * half, -times_i(last, channels))
        spread[:, 2 * half + 1 :] = jnp.zeros_like(spread[:, 2 * half + 1 :])

    def one(i, carry):
        modes_here = spread[step * block + i].reshape(-1, 2 * doubled).astype(jnp.bfloat16)
        left = jnp.concatenate([ty_ref[0], f_ref[i], c_ref[i]], axis=1)
        right = jnp.concatenate([modes_here, mix_ref[...]], axis=0)
        out = jnp.dot(left, right, preferred_element_type=jnp.float32)
        o_ref[i] = out[:, :doubled].astype(jnp.bfloat16)
        b_ref[i] = out[:, doubled:].astype(jnp.bfloat16)
        return carry

    lax.fori_loop(0, block, one, 0)


def whole(shape):
    zeros = (0,) * len(shape)
    return pl.BlockSpec(shape, lambda i, where: zeros)


def one_of(table, axis):
    return pl.BlockSpec((1,) + table.shape[1:], lambda i, where: (where[axis], 0, 0))


def on_device(field, cotangent, spectral_weight, mix_weight):
    x_cells, y_cells, pairs, doubled = field.shape
    channels = doubled // 2
    modes = spectral_weight.shape[0]
    count = spectral_weight.shape[1]
    nx, ny = lax.axis_size("gx"), lax.axis_size("gy")
    total_x, total_y = x_cells * nx, y_cells * ny
    me, core = lax.axis_index("gx"), lax.axis_index("gy")
    tables = make_tables(total_x, total_y, modes, pairs, nx, ny)
    ty_fwd, ty_inv, tx_fwd, tx_inv = [jnp.asarray(t) for t in tables]
    where = jnp.stack([me, core]).astype(jnp.int32)
    flat = (x_cells, y_cells * pairs, doubled)
    field2, cot2 = field.reshape(flat), cotangent.reshape(flat)
    block = 4
    grid = (x_cells // block,)
    data_spec = pl.BlockSpec((block,) + flat[1:], lambda i, where: (i, 0, 0))
    wide = 2 * doubled
    groups = modes * pairs
    params = pltpu.CompilerParams(vmem_limit_bytes=VMEM_LIMIT)

    partial = pl.pallas_call(
        functools.partial(forward_kernel, modes),
        grid_spec=pltpu.PrefetchScalarGridSpec(
            num_scalar_prefetch=1,
            grid=grid,
            in_specs=[data_spec, data_spec, one_of(ty_fwd, 1), one_of(tx_fwd, 0)],
            out_specs=whole((groups, modes, wide)),
            scratch_shapes=[pltpu.VMEM((x_cells, modes, pairs, wide), jnp.float32)],
        ),
        out_shape=jax.ShapeDtypeStruct((groups, modes, wide), jnp.bfloat16),
        compiler_params=params,
        name="forward",
    )(where, field2, cot2, ty_fwd, tx_fwd)

    vmem = pl.BlockSpec(memory_space=pltpu.VMEM)
    hbm = pl.BlockSpec(memory_space=pl.ANY)
    share = (count, modes, wide)
    hosts = nx // 2
    dma = pltpu.SemaphoreType.DMA
    hat, grad_part = pl.pallas_call(
        functools.partial(reduce_kernel, nx),
        out_shape=(
            jax.ShapeDtypeStruct(share, jnp.float32),
            jax.ShapeDtypeStruct((channels, channels), jnp.float32),
        ),
        in_specs=[vmem, hbm, hbm],
        out_specs=(vmem, vmem),
        scratch_shapes=[
            pltpu.VMEM((nx,) + share, jnp.bfloat16),
            pltpu.VMEM((hosts, 2) + share, jnp.bfloat16),
            pltpu.VMEM((hosts,) + share, jnp.bfloat16),
            pltpu.VMEM((hosts,) + share, jnp.bfloat16),
            pltpu.VMEM((2, block) + flat[1:], jnp.bfloat16),
            pltpu.VMEM((2, block) + flat[1:], jnp.bfloat16),
            pltpu.VMEM((doubled, doubled), jnp.float32),
            dma((nx,)), dma((nx,)), dma((hosts,)), dma((hosts,)), dma((hosts,)), dma((hosts,)),
            dma((2,)), dma((2,)),
        ],
        compiler_params=pltpu.CompilerParams(
            collective_id=0, has_side_effects=True, vmem_limit_bytes=VMEM_LIMIT
        ),
        name="reduce",
    )(partial.reshape((nx, ny) + share), field2, cot2)

    hat = jnp.transpose(hat, (1, 0, 2)).astype(jnp.bfloat16).astype(jnp.float32)
    turned = jnp.transpose(hat[:, :, :doubled], (0, 2, 1))
    qb = 4
    z, spectral_grad = pl.pallas_call(
        modes_kernel,
        grid=(modes // qb,),
        out_shape=(
            jax.ShapeDtypeStruct((modes, count, wide), jnp.float32),
            jax.ShapeDtypeStruct((modes, count, channels, doubled), jnp.float32),
        ),
        in_specs=[
            pl.BlockSpec((qb, count, wide), lambda i: (i, 0, 0)),
            pl.BlockSpec((qb, doubled, count), lambda i: (i, 0, 0)),
            pl.BlockSpec((qb, count, channels, doubled), lambda i: (i, 0, 0, 0)),
        ],
        out_specs=(
            pl.BlockSpec((qb, count, wide), lambda i: (i, 0, 0)),
            pl.BlockSpec((qb, count, channels, doubled), lambda i: (i, 0, 0, 0)),
        ),
        compiler_params=params,
        name="modes",
    )(hat, turned, spectral_weight)
    z = jnp.transpose(z, (1, 0, 2)).astype(jnp.bfloat16)

    matrix = pltpu.VMEM((channels, channels), jnp.float32)
    everything, mix_grad = pl.pallas_call(
        functools.partial(
            gather_kernel, nx, 1.0 / math.sqrt(2 * total_x * total_y * pairs)
        ),
        out_shape=(
            jax.ShapeDtypeStruct((nx, ny) + share, jnp.bfloat16),
            jax.ShapeDtypeStruct((channels, channels), jnp.float32),
        ),
        in_specs=[vmem, vmem],
        out_specs=(vmem, vmem),
        scratch_shapes=[
            matrix, matrix, matrix, pltpu.VMEM((hosts, channels, channels), jnp.float32),
            dma((hosts,)), dma((hosts,)), dma((hosts,)), dma((hosts,)), dma((hosts,)),
            dma((nx,)), dma((nx,)), dma, dma, dma, dma, dma((hosts,)), dma((hosts,)),
        ],
        compiler_params=pltpu.CompilerParams(
            collective_id=1, has_side_effects=True, vmem_limit_bytes=VMEM_LIMIT
        ),
        name="gather",
    )(z, grad_part)

    empty = jnp.zeros_like(mix_weight)
    back = mix_weight.T
    rows = [
        [mix_weight if a == b else empty for b in range(2)] + [empty] * 2 for a in range(2)
    ] + [[empty] * 2 + [back if a == b else empty for b in range(2)] for a in range(2)]
    mixing = jnp.block(rows)
    mixed, field_grad = pl.pallas_call(
        functools.partial(inverse_kernel, modes),
        grid_spec=pltpu.PrefetchScalarGridSpec(
            num_scalar_prefetch=1,
            grid=grid,
            in_specs=[
                data_spec, data_spec, whole((groups, modes, wide)),
                one_of(ty_inv, 1), one_of(tx_inv, 0), whole(mixing.shape),
            ],
            out_specs=(data_spec, data_spec),
            scratch_shapes=[pltpu.VMEM((x_cells, SLOTS, pairs, wide), jnp.float32)],
        ),
        out_shape=(jax.ShapeDtypeStruct(flat, jnp.bfloat16),) * 2,
        compiler_params=params,
        name="inverse",
    )(where, field2, cot2, everything.reshape(groups, modes, wide), ty_inv, tx_inv, mixing)
    return (
        mixed.reshape(field.shape), field_grad.reshape(field.shape), spectral_grad, mix_grad
    )


def solution(mesh):
    placed = (
        P(("groups", "gx"), "gy", None, None),
        P(("groups", "gx"), "gy", None, None),
        P(None, ("gx", "gy"), None, None),
        P(),
    )
    return jax.shard_map(
        on_device,
        mesh=mesh,
        in_specs=placed,
        out_specs=(
            P(("groups", "gx"), "gy", None, None),
            P(("groups", "gx"), "gy", None, None),
            P("groups", ("gx", "gy"), None, None),
            P("groups", None),
        ),
        check_vma=False,
    )
```

time: 151 us -> 127 us (0.84)
  the two profiles are of different devices: /device:TPU:29 before, /device:TPU:0 now
where the time goes in v2:
time: 127 us
  Pallas kernels  117 us (92%)
  local copies, waits for them, and re-layouts  8.01 us (6%)
    pallas_call x1, Pallas kernels, on_device(): pl.pallas_call(functools.partial(reduce_kernel, nx), out_shape=(jax.Shape...  26.6 us
    pallas_call x1, Pallas kernels, on_device(): pl.pallas_call(functools.partial(inverse_kernel, modes), grid_spec=pltpu....  25.7 us
    pallas_call x1, Pallas kernels, on_device(): pl.pallas_call(modes_kernel, grid=(modes // qb,), out_shape=(jax.ShapeDty...  22.7 us
    pallas_call x1, Pallas kernels, on_device(): pl.pallas_call(functools.partial(forward_kernel, modes), grid_spec=pltpu....  20.8 us
    pallas_call x1, Pallas kernels, on_device(): pl.pallas_call(functools.partial(gather_kernel, nx, 1.0 / math.sqrt(2 * t...  20.8 us
    unnamed x10, local copies, waits for them, and re-layouts  3.99 us

profile of v2, /device:TPU:0, one launch (start us, length us, event | category | flops | bytes accessed | tf_op | source)
XLA Modules:
  0.0 126.5 jit_solution(3585734208115500752)
XLA Ops:
  0.6 0.1 pad_add_fusion._
  0.7 0.8 copy.15
  1.5 0.9 maximum_maximum_fusion.mix_ref
  2.5 0.0 copy-start.1
  2.5 1.4 %copy-done.1 = bf16[8,384,256]{2,1,0:T(8,128)(2,1)S(1)} copy-done((bf16[8,384,256]{2,1,0:T(8,128)(2,1)S(1)}, bf16[8,384,256]{2,1,0:T(8,128)(2,1)}, u32[]{:S(2)}) %copy-start.1) | copy-done | bytes 1572888
  3.9 0.0 copy-start.3
  3.9 1.2 copy-done.3
  5.0 20.8 %forward.1 = bf16[192,24,256]{2,1,0:T(8,128)(2,1)S(1)} custom-call(s32[2]{0:T(128)S(1)} %pad_add_fusion._, bf16[32,1024,128]{2,1,0:T(8,128)(2,1)} %bitcast.20, bf16[32,1024,128]{2,1,0:T(8,128)(2,1)} %bitcast.23, bf16[2,208,1024]{2,1,0:T(8,128)(2,1)S(1)} %copy-done.3, bf16[8,384,256]{2,1,0:T(8,128)(2,1)S(1)} %copy-done.1), custom_call_target="tpu_custom_call" | custom-call | tf_op jit(solution)/shard_map/forward/pallas_call | solution.py:506
  25.9 26.6 %reduce.1 = (f32[12,24,256]{2,1,0:T(8,128)S(1)}, f32[64,64]{1,0:T(8,128)S(1)}) custom-call(bf16[8,2,12,24,256]{4,3,2,1,0:T(8,128)(2,1)S(1)} %bitcast.17, bf16[32,1024,128]{2,1,0:T(8,128)(2,1)} %bitcast.21, bf16[32,1024,128]{2,1,0:T(8,128)(2,1)} %bitcast.24), custom_call_target="tpu_custom_call" | custom-call | tf_op jit(solution)/shard_map/reduce/pallas_call | solution.py:525
  52.6 0.1 copy.13.hat_ref
  52.7 2.2 %copy.12 = f32[12,24,256]{0,2,1:T(8,128)} copy(f32[12,24,256]{2,1,0:T(8,128)S(1)} %get-tuple-element.20) | data formatting | bytes 589824 | tf_op jit(solution)/shard_map/convert_element_type | solution.py:550
  54.9 1.6 %slice_bitcast_fusion.turned_ref = f32[24,128,12]{2,1,0:T(8,128)S(1)} fusion(f32[24,12,256]{1,2,0:T(8,128)} %bitcast.26), kind=kLoop, calls=%fused_computation | loop fusion | bytes 294912 | tf_op jit(solution)/shard_map/transpose | solution.py:551
  56.4 0.0 copy-start
  56.5 0.0 copy-start.2
  56.5 22.7 %modes.1 = (f32[24,12,256]{2,1,0:T(8,128)S(1)}, f32[24,12,64,128]{3,2,1,0:T(8,128)}) custom-call(f32[24,12,256]{2,1,0:T(8,128)S(1)} %copy.13.hat_ref, f32[24,128,12]{2,1,0:T(8,128)S(1)} %slice_bitcast_fusion.turned_ref, bf16[24,12,64,128]{3,2,1,0:T(8,128)(2,1)} %w_ref.1), custom_call_target="tpu_custom_call" | custom-call | tf_op jit(solution)/shard_map/modes/pallas_call | solution.py:553
  79.2 0.2 copy.20
  79.4 20.8 %gather.1 = (bf16[8,2,12,24,256]{4,3,2,1,0:T(8,128)(2,1)S(1)}, f32[64,64]{1,0:T(8,128)S(1)}) custom-call(bf16[12,24,256]{2,1,0:T(8,128)(2,1)S(1)} %bitcast.19, f32[64,64]{1,0:T(8,128)S(1)} %get-tuple-element.14.g_ref), custom_call_target="tpu_custom_call" | custom-call | tf_op jit(solution)/shard_map/gather/pallas_call | solution.py:575
  100.2 0.0 copy-done
  100.2 0.0 copy-done.2
  100.2 25.7 %inverse.1 = (bf16[32,1024,128]{2,1,0:T(8,128)(2,1)}, bf16[32,1024,128]{2,1,0:T(8,128)(2,1)}) custom-call(s32[2]{0:T(128)S(1)} %pad_add_fusion._, bf16[32,1024,128]{2,1,0:T(8,128)(2,1)} %bitcast.22, bf16[32,1024,128]{2,1,0:T(8,128)(2,1)} %bitcast.25, bf16[192,24,256]{2,1,0:T(8,128)(2,1)S(1)} %bitcast.18, bf16[2,1024,256]{2,1,0:T(8,128)(2,1)S(1)} %copy-done.2, ...), custom_call_target="tpu_custom_call" | custom-call | tf_op jit(solution)/shard_map/inverse/pallas_call | solution.py:602
  125.9 0.6 copy.22
  (2 shorter events, 0.0 us)
Async XLA Ops:
  2.5 1.4 %copy-start.1 = (bf16[8,384,256]{2,1,0:T(8,128)(2,1)S(1)}, bf16[8,384,256]{2,1,0:T(8,128)(2,1)}, u32[]{:S(2)}) copy-start(bf16[8,384,256]{2,1,0:T(8,128)(2,1)} %constant.20.clone.tx_ref) | copy-start | bytes 4718596
  3.9 1.2 copy-start.3
  56.4 43.8 %copy-start = (bf16[8,512,192]{2,1,0:T(8,128)(2,1)S(1)}, bf16[8,512,192]{2,1,0:T(8,128)(2,1)}, u32[]{:S(2)}) copy-start(bf16[8,512,192]{2,1,0:T(8,128)(2,1)} %constant.21.clone.tx_ref) | copy-start | bytes 4718596
  56.5 43.8 %copy-start.2 = (bf16[2,1024,256]{2,1,0:T(8,128)(2,1)S(1)}, bf16[2,1024,256]{2,1,0:T(8,128)(2,1)}, u32[]{:S(2)}) copy-start(bf16[2,1024,256]{2,1,0:T(8,128)(2,1)} %constant.19.clone.ty_ref) | copy-start | bytes 3145732

commit v3 on v2

--- a/solution.py
+++ b/solution.py
@@ -82,7 +82,7 @@
             rows[at, modes - m] = even + odd
         return carry
 
-    lax.fori_loop(0, block, one, 0)
+    lax.fori_loop(0, block, one, 0, unroll=4)
 
     @pl.when(step == pl.num_programs(0) - 1)
     def _():
@@ -96,7 +96,7 @@
             )
             return carry
 
-        lax.fori_loop(0, modes, mode, 0)
+        lax.fori_loop(0, modes, mode, 0, unroll=8)
 
 
 def barrier_with(n, me, core):
@@ -261,7 +261,7 @@
     high, low = me // 2, lax.rem(me, 2)
     partner = high * 2 + 1 - low
     barrier_with(n, me, core)
-    all_ref[me, core] = z_ref[...]
+    all_ref[me, core] = z_ref[...].astype(jnp.bfloat16)
 
     def along(h, step, sems):
         block = all_ref.at[h * 2 + low, core]
@@ -402,30 +402,64 @@
     mix_ref[...] = mix * scale
 
 
-def modes_kernel(hat_ref, turned_ref, w_ref, z_ref, grad_ref):
+def modes_kernel(hat_ref, w_ref, z_ref, grad_ref):
     block, count, channels, doubled = w_ref.shape
-    rows = lax.broadcasted_iota(jnp.int32, (8, doubled), 0)
-
-    def one(i, carry):
+    padded = -(-count // 8) * 8
+    shape = (2 * padded, doubled)
+    row = lax.broadcasted_iota(jnp.int32, shape, 0)
+    lane = lax.broadcasted_iota(jnp.int32, shape, 1)
+    pair = jnp.where(row >= padded, row - padded, row)
+    right = (lane >= channels).astype(jnp.int32)
+    left = lane[:padded] < channels
+    tiles = -(-count // 2)
+
+    for i in range(block):
+        lines = [hat_ref[g, i : i + 1, :] for g in range(count)]
+        if padded > count:
+            lines.append(jnp.zeros((padded - count, 2 * doubled), jnp.float32))
+        lines = jnp.concatenate(lines, axis=0)
+        f, c = lines[:, :doubled], lines[:, doubled:]
+        swapped = pltpu.roll(f, channels, 1)
+        hat = jnp.concatenate(
+            [jnp.where(left, f, swapped), jnp.where(left, swapped, f)], axis=0
+        )
+        cot = jnp.concatenate([c, -times_i(c, channels)], axis=0)
+        weight = w_ref[i].reshape(count * channels, doubled)
+
+        spaced = jnp.concatenate(
+            [jnp.where(pair == 2 * t + right, hat, 0.0) for t in range(tiles)], axis=1
+        )[:, : count * channels]
+        both = jnp.dot(
+            spaced.astype(jnp.bfloat16), weight, preferred_element_type=jnp.float32
+        )
+        out = both[:padded] + times_i(both[padded:], channels)
+
+        every = lax.dot_general(
+            cot.astype(jnp.bfloat16), weight, (((1,), (1,)), ((), ())),
+            preferred_element_type=jnp.float32,
+        )
+        if count % 2:
+            every = jnp.concatenate(
+                [every, jnp.zeros((2 * padded, channels), jnp.float32)], axis=1
+            )
+        own = jnp.zeros(shape, jnp.float32)
+        for t in range(tiles):
+            tile = every[:, t * doubled : (t + 1) * doubled]
+            own = own + jnp.where(pair == 2 * t + right, tile, 0.0)
+        own = own + pltpu.roll(own, channels, 1)
+        back = jnp.where(left, own[:padded], own[padded:])
+
+        columns = jnp.transpose(hat)[:channels].astype(jnp.bfloat16)
+        spread = jnp.concatenate(
+            [jnp.where(pair == g, cot, 0.0) for g in range(count)], axis=1
+        )
+        grad = jnp.dot(
+            columns, spread.astype(jnp.bfloat16), preferred_element_type=jnp.float32
+        )
         for g in range(count):
-            cot = hat_ref[i, g : g + 1, doubled:]
-            turned = -times_i(cot, channels)
-            real = turned_ref[i, :channels, g : g + 1]
-            imag = turned_ref[i, channels:doubled, g : g + 1]
-            weight16 = w_ref[i, g]
-            weight = weight16.astype(jnp.float32)
-            grad_ref[i, g] = real * cot + imag * turned
-            first = jnp.sum(real * weight, axis=0, keepdims=True)
-            second = jnp.sum(imag * weight, axis=0, keepdims=True)
-            z_ref[i, g : g + 1, :doubled] = first + times_i(second, channels)
-            sides = jnp.where(rows == 0, cot, turned).astype(jnp.bfloat16)
-            back = lax.dot_general(
-                sides, weight16, (((1,), (1,)), ((), ())), preferred_element_type=jnp.float32
-            )
-            z_ref[i, g : g + 1, doubled:] = jnp.concatenate([back[0:1], back[1:2]], axis=1)
-        return carry
-
-    lax.fori_loop(0, block, one, 0)
+            grad_ref[i, g] = grad[:, g * doubled : (g + 1) * doubled]
+            z_ref[g, i : i + 1, :doubled] = out[g : g + 1]
+            z_ref[g, i : i + 1, doubled:] = back[g : g + 1]
 
 
 def inverse_kernel(modes, _, f_ref, c_ref, z_ref, ty_ref, tx_ref, mix_ref, o_ref, b_ref, spread):
@@ -456,7 +490,7 @@
             put(half + m, times_i(plus - minus, channels))
             return carry
 
-        lax.fori_loop(1, half, pair, 0)
+        lax.fori_loop(1, half, pair, 0, unroll=6)
         last = expand(half)
         put(half, last)
         put(2 * half, -times_i(last, channels))
@@ -471,7 +505,7 @@
         b_ref[i] = out[:, doubled:].astype(jnp.bfloat16)
         return carry
 
-    lax.fori_loop(0, block, one, 0)
+    lax.fori_loop(0, block, one, 0, unroll=4)
 
 
 def whole(shape):
@@ -547,29 +581,25 @@
         name="reduce",
     )(partial.reshape((nx, ny) + share), field2, cot2)
 
-    hat = jnp.transpose(hat, (1, 0, 2)).astype(jnp.bfloat16).astype(jnp.float32)
-    turned = jnp.transpose(hat[:, :, :doubled], (0, 2, 1))
-    qb = 4
+    qb = 8
     z, spectral_grad = pl.pallas_call(
         modes_kernel,
         grid=(modes // qb,),
         out_shape=(
-            jax.ShapeDtypeStruct((modes, count, wide), jnp.float32),
+            jax.ShapeDtypeStruct(share, jnp.float32),
             jax.ShapeDtypeStruct((modes, count, channels, doubled), jnp.float32),
         ),
         in_specs=[
-            pl.BlockSpec((qb, count, wide), lambda i: (i, 0, 0)),
-            pl.BlockSpec((qb, doubled, count), lambda i: (i, 0, 0)),
+            pl.BlockSpec((count, qb, wide), lambda i: (0, i, 0)),
             pl.BlockSpec((qb, count, channels, doubled), lambda i: (i, 0, 0, 0)),
         ],
         out_specs=(
-            pl.BlockSpec((qb, count, wide), lambda i: (i, 0, 0)),
+            pl.BlockSpec((count, qb, wide), lambda i: (0, i, 0)),
             pl.BlockSpec((qb, count, channels, doubled), lambda i: (i, 0, 0, 0)),
         ),
         compiler_params=params,
         name="modes",
-    )(hat, turned, spectral_weight)
-    z = jnp.transpose(z, (1, 0, 2)).astype(jnp.bfloat16)
+    )(hat, spectral_weight)
 
     matrix = pltpu.VMEM((channels, channels), jnp.float32)
     everything, mix_grad = pl.pallas_call(

time: 127 us -> 94.6 us (0.74)
  Pallas kernels: 117 us -> 88.4 us
  local copies, waits for them, and re-layouts: 8.01 us -> 4 us
    pallas_call x1, Pallas kernels: 22.7 us -> 6.07 us  [on_device(): pl.pallas_call(modes_kernel, grid=(modes // qb,), out_shape=(jax.ShapeDty...]
    pallas_call x1, Pallas kernels: 20.8 us -> 13 us  [on_device(): pl.pallas_call(functools.partial(forward_kernel, modes), grid_spec=pltpu....]
    pallas_call x1, Pallas kernels: 25.7 us -> 22 us  [on_device(): pl.pallas_call(functools.partial(inverse_kernel, modes), grid_spec=pltpu....]
    convert_element_type x2 -> x0, local copies, waits for them, and re-layouts: 2.3 us -> none  [on_device(): hat = jnp.transpose(hat, (1, 0, 2)).astype(jnp.bfloat16).astype(jnp.float32)]
    transpose x1 -> x0, local copies, waits for them, and re-layouts: 1.55 us -> none  [on_device(): turned = jnp.transpose(hat[:, :, :doubled], (0, 2, 1))]
    unnamed x10 -> x12, local copies, waits for them, and re-layouts: 3.99 us -> 3.99 us
where the time goes in v3:
time: 94.6 us; the launch traced here: 94.1 us
  Pallas kernels  88.4 us (93%)
  local copies, waits for them, and re-layouts  4 us (4%)
  other arithmetic  0.99 us (1%)
    pallas_call x1, Pallas kernels, on_device(): pl.pallas_call(functools.partial(reduce_kernel, nx), out_shape=(jax.Shape...  26.6 us
    pallas_call x1, Pallas kernels, on_device(): pl.pallas_call(functools.partial(inverse_kernel, modes), grid_spec=pltpu....  22 us
    pallas_call x1, Pallas kernels, on_device(): pl.pallas_call(functools.partial(gather_kernel, nx, 1.0 / math.sqrt(2 * t...  20.7 us
    pallas_call x1, Pallas kernels, on_device(): pl.pallas_call(functools.partial(forward_kernel, modes), grid_spec=pltpu....  13 us
    pallas_call x1, Pallas kernels, on_device(): pl.pallas_call(modes_kernel, grid=(modes // qb,), out_shape=(jax.ShapeDty...  6.07 us
    unnamed x12, local copies, waits for them, and re-layouts  3.99 us

profile of v3, /device:TPU:0, one launch (start us, length us, event | category | flops | bytes accessed | tf_op | source)
XLA Modules:
  0.0 94.1 jit_solution(7984695985903665026)
XLA Ops:
  0.6 0.1 pad_add_fusion._
  0.7 0.8 copy.12
  1.5 0.9 maximum_maximum_fusion.mix_ref
  2.5 0.0 copy-start.2
  2.5 1.4 %copy-done.2 = bf16[8,384,256]{2,1,0:T(8,128)(2,1)S(1)} copy-done((bf16[8,384,256]{2,1,0:T(8,128)(2,1)S(1)}, bf16[8,384,256]{2,1,0:T(8,128)(2,1)}, u32[]{:S(2)}) %copy-start.2) | copy-done | bytes 1572888
  3.9 0.0 copy-start.4
  3.9 1.2 %copy-done.4 = bf16[2,208,1024]{2,1,0:T(8,128)(2,1)S(1)} copy-done((bf16[2,208,1024]{2,1,0:T(8,128)(2,1)S(1)}, bf16[2,208,1024]{2,1,0:T(8,128)(2,1)}, u32[]{:S(2)}) %copy-start.4) | copy-done | bytes 851992
  5.0 13.0 %forward.1 = bf16[192,24,256]{2,1,0:T(8,128)(2,1)S(1)} custom-call(s32[2]{0:T(128)S(1)} %pad_add_fusion._, bf16[32,1024,128]{2,1,0:T(8,128)(2,1)} %bitcast.11, bf16[32,1024,128]{2,1,0:T(8,128)(2,1)} %bitcast.14, bf16[2,208,1024]{2,1,0:T(8,128)(2,1)S(1)} %copy-done.4, bf16[8,384,256]{2,1,0:T(8,128)(2,1)S(1)} %copy-done.2), custom_call_target="tpu_custom_call" | custom-call | tf_op jit(solution)/shard_map/forward/pallas_call | solution.py:540
  18.0 0.0 copy-start
  18.0 0.0 copy-start.1
  18.0 0.0 copy-start.3
  18.0 26.6 %reduce.1 = (f32[12,24,256]{2,1,0:T(8,128)S(1)}, f32[64,64]{1,0:T(8,128)S(1)}) custom-call(bf16[8,2,12,24,256]{4,3,2,1,0:T(8,128)(2,1)S(1)} %bitcast.9, bf16[32,1024,128]{2,1,0:T(8,128)(2,1)} %bitcast.12, bf16[32,1024,128]{2,1,0:T(8,128)(2,1)} %bitcast.15), custom_call_target="tpu_custom_call" | custom-call | tf_op jit(solution)/shard_map/reduce/pallas_call | solution.py:559
  44.7 0.0 copy-done
  44.7 6.1 %modes.1 = (f32[12,24,256]{2,1,0:T(8,128)S(1)}, f32[24,12,64,128]{3,2,1,0:T(8,128)}) custom-call(f32[12,24,256]{2,1,0:T(8,128)S(1)} %get-tuple-element.12.hat_ref, bf16[24,12,64,128]{3,2,1,0:T(8,128)(2,1)S(1)} %copy-done), custom_call_target="tpu_custom_call" | custom-call | tf_op jit(solution)/shard_map/modes/pallas_call | solution.py:585
  50.7 20.7 %gather.1 = (bf16[8,2,12,24,256]{4,3,2,1,0:T(8,128)(2,1)S(1)}, f32[64,64]{1,0:T(8,128)S(1)}) custom-call(f32[12,24,256]{2,1,0:T(8,128)S(1)} %get-tuple-element.13.z_ref, f32[64,64]{1,0:T(8,128)S(1)} %get-tuple-element.14.g_ref), custom_call_target="tpu_custom_call" | custom-call | tf_op jit(solution)/shard_map/gather/pallas_call | solution.py:605
  71.5 0.0 copy-done.1
  71.5 0.0 copy-done.3
  71.5 22.0 %inverse.1 = (bf16[32,1024,128]{2,1,0:T(8,128)(2,1)}, bf16[32,1024,128]{2,1,0:T(8,128)(2,1)}) custom-call(s32[2]{0:T(128)S(1)} %pad_add_fusion._, bf16[32,1024,128]{2,1,0:T(8,128)(2,1)} %bitcast.13, bf16[32,1024,128]{2,1,0:T(8,128)(2,1)} %bitcast.16, bf16[192,24,256]{2,1,0:T(8,128)(2,1)S(1)} %bitcast.10, bf16[2,1024,256]{2,1,0:T(8,128)(2,1)S(1)} %copy-done.3, ...), custom_call_target="tpu_custom_call" | custom-call | tf_op jit(solution)/shard_map/inverse/pallas_call | solution.py:632
  93.5 0.6 copy.14
  (1 shorter events, 0.0 us)
Async XLA Ops:
  2.5 1.4 %copy-start.2 = (bf16[8,384,256]{2,1,0:T(8,128)(2,1)S(1)}, bf16[8,384,256]{2,1,0:T(8,128)(2,1)}, u32[]{:S(2)}) copy-start(bf16[8,384,256]{2,1,0:T(8,128)(2,1)} %constant.20.clone.tx_ref) | copy-start | bytes 4718596
  3.9 1.2 %copy-start.4 = (bf16[2,208,1024]{2,1,0:T(8,128)(2,1)S(1)}, bf16[2,208,1024]{2,1,0:T(8,128)(2,1)}, u32[]{:S(2)}) copy-start(bf16[2,208,1024]{2,1,0:T(8,128)(2,1)} %constant.18.clone.ty_ref) | copy-start | bytes 2555908
  18.0 26.7 %copy-start = (bf16[24,12,64,128]{3,2,1,0:T(8,128)(2,1)S(1)}, bf16[24,12,64,128]{3,2,1,0:T(8,128)(2,1)}, u32[]{:S(2)}) copy-start(bf16[24,12,64,128]{3,2,1,0:T(8,128)(2,1)} %w_ref.1) | copy-start | bytes 14155780
  18.0 53.5 %copy-start.1 = (bf16[8,512,192]{2,1,0:T(8,128)(2,1)S(1)}, bf16[8,512,192]{2,1,0:T(8,128)(2,1)}, u32[]{:S(2)}) copy-start(bf16[8,512,192]{2,1,0:T(8,128)(2,1)} %constant.21.clone.tx_ref) | copy-start | bytes 4718596
  18.0 53.5 %copy-start.3 = (bf16[2,1024,256]{2,1,0:T(8,128)(2,1)S(1)}, bf16[2,1024,256]{2,1,0:T(8,128)(2,1)}, u32[]{:S(2)}) copy-start(bf16[2,1024,256]{2,1,0:T(8,128)(2,1)} %constant.19.clone.ty_ref) | copy-start | bytes 3145732

commit v4 on v3

--- a/solution.py
+++ b/solution.py
@@ -96,7 +96,7 @@
             )
             return carry
 
-        lax.fori_loop(0, modes, mode, 0, unroll=8)
+        lax.fori_loop(0, modes, mode, 0, unroll=modes)
 
 
 def barrier_with(n, me, core):
@@ -490,7 +490,7 @@
             put(half + m, times_i(plus - minus, channels))
             return carry
 
-        lax.fori_loop(1, half, pair, 0, unroll=6)
+        lax.fori_loop(1, half, pair, 0, unroll=half - 1)
         last = expand(half)
         put(half, last)
         put(2 * half, -times_i(last, channels))

time: 94.6 us -> 92.5 us (0.978)
  Pallas kernels: 88.4 us -> 86.2 us
    pallas_call x1, Pallas kernels: 22 us -> 20.4 us  [on_device(): pl.pallas_call(functools.partial(inverse_kernel, modes), grid_spec=pltpu....]
where the time goes in v4:
time: 92.5 us; the launch traced here: 91.9 us
  Pallas kernels  86.2 us (93%)
  local copies, waits for them, and re-layouts  4 us (4%)
  other arithmetic  0.99 us (1%)
    pallas_call x1, Pallas kernels, on_device(): pl.pallas_call(functools.partial(reduce_kernel, nx), out_shape=(jax.Shape...  26.6 us
    pallas_call x1, Pallas kernels, on_device(): pl.pallas_call(functools.partial(gather_kernel, nx, 1.0 / math.sqrt(2 * t...  20.7 us
    pallas_call x1, Pallas kernels, on_device(): pl.pallas_call(functools.partial(inverse_kernel, modes), grid_spec=pltpu....  20.4 us
    pallas_call x1, Pallas kernels, on_device(): pl.pallas_call(functools.partial(forward_kernel, modes), grid_spec=pltpu....  12.4 us
    pallas_call x1, Pallas kernels, on_device(): pl.pallas_call(modes_kernel, grid=(modes // qb,), out_shape=(jax.ShapeDty...  6.07 us
    unnamed x12, local copies, waits for them, and re-layouts  3.99 us

profile of v4, /device:TPU:0, one launch (start us, length us, event | category | flops | bytes accessed | tf_op | source)
XLA Modules:
  0.0 91.9 jit_solution(14466519768681270850)
XLA Ops:
  0.6 0.1 pad_add_fusion._
  0.7 0.8 copy.12
  1.5 0.9 maximum_maximum_fusion.mix_ref
  2.5 0.0 copy-start.2
  2.5 1.4 %copy-done.2 = bf16[8,384,256]{2,1,0:T(8,128)(2,1)S(1)} copy-done((bf16[8,384,256]{2,1,0:T(8,128)(2,1)S(1)}, bf16[8,384,256]{2,1,0:T(8,128)(2,1)}, u32[]{:S(2)}) %copy-start.2) | copy-done | bytes 1572888
  3.9 0.0 copy-start.4
  3.9 1.2 %copy-done.4 = bf16[2,208,1024]{2,1,0:T(8,128)(2,1)S(1)} copy-done((bf16[2,208,1024]{2,1,0:T(8,128)(2,1)S(1)}, bf16[2,208,1024]{2,1,0:T(8,128)(2,1)}, u32[]{:S(2)}) %copy-start.4) | copy-done | bytes 851992
  5.0 12.4 %forward.1 = bf16[192,24,256]{2,1,0:T(8,128)(2,1)S(1)} custom-call(s32[2]{0:T(128)S(1)} %pad_add_fusion._, bf16[32,1024,128]{2,1,0:T(8,128)(2,1)} %bitcast.11, bf16[32,1024,128]{2,1,0:T(8,128)(2,1)} %bitcast.14, bf16[2,208,1024]{2,1,0:T(8,128)(2,1)S(1)} %copy-done.4, bf16[8,384,256]{2,1,0:T(8,128)(2,1)S(1)} %copy-done.2), custom_call_target="tpu_custom_call" | custom-call | tf_op jit(solution)/shard_map/forward/pallas_call | solution.py:540
  17.4 0.0 copy-start
  17.4 0.0 copy-start.1
  17.5 0.0 copy-start.3
  17.5 26.6 %reduce.1 = (f32[12,24,256]{2,1,0:T(8,128)S(1)}, f32[64,64]{1,0:T(8,128)S(1)}) custom-call(bf16[8,2,12,24,256]{4,3,2,1,0:T(8,128)(2,1)S(1)} %bitcast.9, bf16[32,1024,128]{2,1,0:T(8,128)(2,1)} %bitcast.12, bf16[32,1024,128]{2,1,0:T(8,128)(2,1)} %bitcast.15), custom_call_target="tpu_custom_call" | custom-call | tf_op jit(solution)/shard_map/reduce/pallas_call | solution.py:559
  44.1 0.0 copy-done
  44.1 6.1 %modes.1 = (f32[12,24,256]{2,1,0:T(8,128)S(1)}, f32[24,12,64,128]{3,2,1,0:T(8,128)}) custom-call(f32[12,24,256]{2,1,0:T(8,128)S(1)} %get-tuple-element.12.hat_ref, bf16[24,12,64,128]{3,2,1,0:T(8,128)(2,1)S(1)} %copy-done), custom_call_target="tpu_custom_call" | custom-call | tf_op jit(solution)/shard_map/modes/pallas_call | solution.py:585
  50.2 20.7 %gather.1 = (bf16[8,2,12,24,256]{4,3,2,1,0:T(8,128)(2,1)S(1)}, f32[64,64]{1,0:T(8,128)S(1)}) custom-call(f32[12,24,256]{2,1,0:T(8,128)S(1)} %get-tuple-element.13.z_ref, f32[64,64]{1,0:T(8,128)S(1)} %get-tuple-element.14.g_ref), custom_call_target="tpu_custom_call" | custom-call | tf_op jit(solution)/shard_map/gather/pallas_call | solution.py:605
  70.9 0.0 copy-done.1
  70.9 0.0 copy-done.3
  70.9 20.4 %inverse.1 = (bf16[32,1024,128]{2,1,0:T(8,128)(2,1)}, bf16[32,1024,128]{2,1,0:T(8,128)(2,1)}) custom-call(s32[2]{0:T(128)S(1)} %pad_add_fusion._, bf16[32,1024,128]{2,1,0:T(8,128)(2,1)} %bitcast.13, bf16[32,1024,128]{2,1,0:T(8,128)(2,1)} %bitcast.16, bf16[192,24,256]{2,1,0:T(8,128)(2,1)S(1)} %bitcast.10, bf16[2,1024,256]{2,1,0:T(8,128)(2,1)S(1)} %copy-done.3, ...), custom_call_target="tpu_custom_call" | custom-call | tf_op jit(solution)/shard_map/inverse/pallas_call | solution.py:632
  91.3 0.6 copy.14
  (1 shorter events, 0.0 us)
Async XLA Ops:
  2.5 1.4 %copy-start.2 = (bf16[8,384,256]{2,1,0:T(8,128)(2,1)S(1)}, bf16[8,384,256]{2,1,0:T(8,128)(2,1)}, u32[]{:S(2)}) copy-start(bf16[8,384,256]{2,1,0:T(8,128)(2,1)} %constant.20.clone.tx_ref) | copy-start | bytes 4718596
  3.9 1.2 %copy-start.4 = (bf16[2,208,1024]{2,1,0:T(8,128)(2,1)S(1)}, bf16[2,208,1024]{2,1,0:T(8,128)(2,1)}, u32[]{:S(2)}) copy-start(bf16[2,208,1024]{2,1,0:T(8,128)(2,1)} %constant.18.clone.ty_ref) | copy-start | bytes 2555908
  17.4 26.7 %copy-start = (bf16[24,12,64,128]{3,2,1,0:T(8,128)(2,1)S(1)}, bf16[24,12,64,128]{3,2,1,0:T(8,128)(2,1)}, u32[]{:S(2)}) copy-start(bf16[24,12,64,128]{3,2,1,0:T(8,128)(2,1)} %w_ref.1) | copy-start | bytes 14155780
  17.4 53.4 %copy-start.1 = (bf16[8,512,192]{2,1,0:T(8,128)(2,1)S(1)}, bf16[8,512,192]{2,1,0:T(8,128)(2,1)}, u32[]{:S(2)}) copy-start(bf16[8,512,192]{2,1,0:T(8,128)(2,1)} %constant.21.clone.tx_ref) | copy-start | bytes 4718596
  17.5 53.4 %copy-start.3 = (bf16[2,1024,256]{2,1,0:T(8,128)(2,1)S(1)}, bf16[2,1024,256]{2,1,0:T(8,128)(2,1)}, u32[]{:S(2)}) copy-start(bf16[2,1024,256]{2,1,0:T(8,128)(2,1)} %constant.19.clone.ty_ref) | copy-start | bytes 3145732
